TPU v7x, 512 devices: a whole 4x8x8 slice. The times are simulated.
512 devices in a mesh: tm: 16 (over y, x_hi), space: 32 (over z, x_lo, core).
Axes of the slice: x: 4 (x_hi: 2, x_lo: 2; x = x_hi * 2 + x_lo), y: 8, z: 8, core: 2. Of those that a mesh axis runs over, the one named last changes fastest.
Arguments:
- start_states: float32 [16, 3, 512, 2048], P('tm', None, 'space'), may hold values from -4 to 4
- lift_weight: float32 [256, 3], replicated, may hold values from -6 to 6
- lift_bias: float32 [256], replicated, may hold values from -3 to 3
- conv_weight: bfloat16 [3, 3, 256, 256], replicated, may hold values from -0.125 to 0.125
- conv_bias: float32 [256], replicated, may hold values from -3 to 3
- out_weight: bfloat16 [3, 256], replicated, may hold values from -0.1875 to 0.1875
Outputs:
- corrected: float32 [16, 3, 512, 2048], P('tm', None, 'space')
All inputs are finite; a program needn't handle non-finite values.
Results may differ from a plain program's by a relative error of at most 0.017.
Values sent between devices are 32-bit elements; how exact they have to be, the bound alone decides.
No kernel may reach another device: no remote copies, remote signals or barrier semaphores. Data moves between devices by JAX's collectives and lax.ppermute only.
A program may use at most 64 MiB of HBM per device.

v0:
```python
import jax
import jax.numpy as jnp
from jax import lax
from jax.sharding import PartitionSpec as P

FINE = 4
RF = 8


time_step = 0.2
viscosity = 1.0
sound_sq = 1.0


def padded(cells, sides, width):
    for axis, dim in sides:
        count = lax.axis_size(axis)
        head = lax.slice_in_dim(cells, 0, width, axis=dim)
        tail = lax.slice_in_dim(cells, cells.shape[dim] - width, cells.shape[dim], axis=dim)
        cells = jnp.concatenate(
            [
                lax.ppermute(tail, axis, [(i, (i + 1) % count) for i in range(count)]),
                cells,
                lax.ppermute(head, axis, [((i + 1) % count, i) for i in range(count)]),
            ],
            axis=dim,
        )
    return cells


def passed_along(value, axis, steps):
    count = lax.axis_size(axis)
    initial, last = (max(0, -steps), min(count, count - steps))
    return lax.ppermute(value, axis, [(source, source + steps) for source in range(initial, last)])


def fine_step(extended):
    center = extended[:, 1:-1, :]
    north = extended[:, :-2, :]
    south = extended[:, 2:, :]
    east = jnp.roll(center, -1, axis=2)
    west = jnp.roll(center, 1, axis=2)
    along_x = (east - west) * 0.5
    along_y = (south - north) * 0.5
    laplace = east + west + north + south - 4.0 * center
    speed_x = center[0]
    speed_y = center[1]
    new_x = speed_x + time_step * (
        -(speed_x * along_x[0] + speed_y * along_y[0]) - along_x[2] + viscosity * laplace[0]
    )
    new_y = speed_y + time_step * (
        -(speed_x * along_x[1] + speed_y * along_y[1]) - along_y[2] + viscosity * laplace[1]
    )
    new_p = (
        center[2]
        - time_step * sound_sq * (along_x[0] + along_y[1])
        + time_step * viscosity * laplace[2]
    )
    return jnp.stack([new_x, new_y, new_p])


def restrict(state_slab):
    fields, rows, columns = state_slab.shape
    return state_slab.reshape(fields, rows // RF, RF, columns // RF, RF).mean(axis=(2, 4))


def prolong(coarse):
    return jnp.repeat(jnp.repeat(coarse, RF, axis=1), RF, axis=2)


def extend_coarse(coarse):
    return padded(coarse, (("space", 1),), 1)


def apply_net(
    extended, lift_weight, lift_bias, conv_weight, conv_bias, out_weight, padded_columns=False
):
    rows = extended.shape[1] - 2
    columns = extended.shape[2]
    channels = conv_weight.shape[2]
    lifted = lift_bias[:, None, None] + lift_weight[:, 0, None, None] * extended[0]
    lifted = (
        lifted
        + lift_weight[:, 1, None, None] * extended[1]
        + lift_weight[:, 2, None, None] * extended[2]
    )
    hidden = jax.nn.gelu(lifted).astype(jnp.bfloat16)
    accumulated = jnp.zeros((channels, rows * columns), jnp.float32)
    for row_tap in range(3):
        for col_tap in range(3):
            shifted = jnp.roll(hidden[:, row_tap : row_tap + rows, :], 1 - col_tap, axis=2)
            accumulated = accumulated + jnp.dot(
                conv_weight[row_tap, col_tap],
                shifted.reshape(channels, rows * columns),
                preferred_element_type=jnp.float32,
            )
    activated = jax.nn.gelu(accumulated + conv_bias[:, None]).astype(jnp.bfloat16)
    increment = jnp.dot(out_weight, activated, preferred_element_type=jnp.float32)
    return extended[:, 1:-1, :] + increment.reshape(3, rows, columns)


def shards(start_states, lift_weight, lift_bias, conv_weight, conv_bias, out_weight):
    weights = (lift_weight, lift_bias, conv_weight, conv_bias, out_weight)
    state_slab = start_states[0]
    fine_end = state_slab
    for repeat in range(FINE):
        fine_end = fine_step(padded(fine_end, (("space", 1),), 1))
    initial = restrict(state_slab)
    guess = apply_net(extend_coarse(initial), *weights)
    correction = fine_end - prolong(guess)
    coarse_correction = restrict(correction)
    slice_index = lax.axis_index("tm")
    slice_count = lax.axis_size("tm")

    def chain_step(turn_index, carried):
        coarse, own_in_loop = carried
        extended = extend_coarse(coarse)

        def active(extended_in, coarse_in, own_in):
            advanced = apply_net(extended_in, *weights)
            return (advanced + coarse_correction, advanced)

        def passive(extended_in, coarse_in, own_in):
            return (coarse_in, own_in)

        passed, own_in_loop = lax.cond(
            slice_index == turn_index, active, passive, extended, coarse, own_in_loop
        )
        return (passed_along(passed, "tm", 1), own_in_loop)

    carried = lax.fori_loop(0, slice_count, chain_step, (initial, jnp.zeros_like(initial)))
    own_coarse = carried[1]
    return (prolong(own_coarse) + correction)[None]


def solution(mesh):
    return jax.shard_map(
        shards,
        mesh=mesh,
        in_specs=(P("tm", None, "space", None), P(), P(), P(), P(), P()),
        out_specs=P("tm", None, "space", None),
        check_vma=False,
    )
```

profile of v0, /device:TPU:60, one launch (start us, length us, event | category | flops | bytes accessed | tf_op | source)
XLA Modules:
  0.0 497.0 jit_solution(2692996376665325467)
XLA Ops:
  0.0 5.9 %reshape_squeeze.3 = f32[3,2,8,256,8]{4,3,2,1,0:T(8,128)} reshape(f32[1,3,16,2048]{3,2,1,0:T(8,128)} %param.10) | data formatting | bytes 786432 | tf_op jit(solution)/shard_map/reshape;squeeze | solution.py:64
  5.9 3.3 reduce_sum.21
  11.2 11.0 %collective-permute-start.12 = (f32[3,1,256]{2,1,0:T(1,128)S(1)}, f32[3,1,256]{2,1,0:T(1,128)S(1)}, u32[]{:S(2)}, u32[]{:S(2)}) collective-permute-start(f32[3,1,256]{2,1,0:T(1,128)S(1)} %get-tuple-element.322), channel_id=1, source_target_pairs={{1,0},{2,1},{3,2},{4,3},{5,4},{6,5},{7,6},{8,7},{9,8},{10,9},{11,1... | collective-permute-start | bytes 9224 | tf_op jit(solution)/shard_map/ppermute | solution.py:24
  22.9 2.6 collective-permute-start.3
  41.2 5.8 %collective-permute-start.5 = (f32[3,1,2048]{2,1,0:T(1,128)S(1)}, f32[3,1,2048]{2,1,0:T(1,128)S(1)}, u32[]{:S(2)}, u32[]{:S(2)}) collective-permute-start(f32[3,1,2048]{2,1,0:T(1,128)S(1)} %get-tuple-element.307), channel_id=1, source_target_pairs={{1,0},{2,1},{3,2},{4,3},{5,4},{6,5},{7,6},{8,7},{9,8},{10,9},{11,1... | collective-permute-start | bytes 73736 | tf_op jit(solution)/shard_map/ppermute | solution.py:24
  49.2 5.1 %collective-permute-done.6 = f32[3,1,2048]{2,1,0:T(1,128)S(1)} collective-permute-done((f32[3,1,2048]{2,1,0:T(1,128)S(1)}, f32[3,1,2048]{2,1,0:T(1,128)S(1)}, u32[]{:S(2)}, u32[]{:S(2)}) %collective-permute-start.6) | collective-permute-done | bytes 24608 | tf_op jit(solution)/shard_map/ppermute | solution.py:22
  56.9 2.4 collective-permute-start.8
  59.4 4.8 collective-permute-done.8
  66.9 5.8 %collective-permute-start.9 = (f32[3,1,2048]{2,1,0:T(1,128)S(1)}, f32[3,1,2048]{2,1,0:T(1,128)S(1)}, u32[]{:S(2)}, u32[]{:S(2)}) collective-permute-start(f32[3,1,2048]{2,1,0:T(1,128)S(1)} %get-tuple-element.295), channel_id=1, source_target_pairs={{1,0},{2,1},{3,2},{4,3},{5,4},{6,5},{7,6},{8,7},{9,8},{10,9},{11,1... | collective-permute-start | bytes 73736 | tf_op jit(solution)/shard_map/ppermute | solution.py:24
  77.0 410.6 %while.15 = (s32[]{:T(128)}, f32[3,2,256]{2,1,0:T(2,128)S(1)}, f32[3,2,256]{2,1,0:T(2,128)S(1)}, s32[]{:T(128)}, f32[256]{0:T(256)S(1)}, /*index=5*/f32[256,3]{0...) while((s32[]{:T(128)}, f32[3,2,256]{2,1,0:T(2,128)S(1)}, ...), condition=%wide.region_6.7_spmd, body=%wide.region_3.6_spmd.sunk | while | flops 614212608 | bytes 25232716 | solution.py:131
  77.0 5.7 %collective-permute-start = (f32[3,1,256]{2,1,0:T(1,128)S(1)}, f32[3,1,256]{2,1,0:T(1,128)S(1)}, u32[]{:S(2)}, u32[]{:S(2)}) collective-permute-start(f32[3,1,256]{2,1,0:T(1,128)S(1)} %get-tuple-element.397), channel_id=1, source_target_pairs={{1,0},{2,1},{3,2},{4,3},{5,4},{6,5},{7,6},{8,7},{9,8},{10,9},{11,1... | collective-permute-start | bytes 9224 | tf_op jit(solution)/shard_map/while/body/eval_jaxpr/ppermute | solution.py:24
  84.8 5.1 %collective-permute-done.1 = f32[3,1,256]{2,1,0:T(1,128)S(1)} collective-permute-done((f32[3,1,256]{2,1,0:T(1,128)S(1)}, f32[3,1,256]{2,1,0:T(1,128)S(1)}, u32[]{:S(2)}, u32[]{:S(2)}) %collective-permute-start.1) | collective-permute-done | bytes 3104 | tf_op jit(solution)/shard_map/while/body/eval_jaxpr/ppermute | solution.py:22
  91.2 5.7 %collective-permute-done.2 = f32[3,2,256]{2,1,0:T(2,128)S(1)} collective-permute-done((f32[3,2,256]{2,1,0:T(2,128)S(1)}, f32[3,2,256]{2,1,0:T(2,128)S(1)}, u32[]{:S(2)}, u32[]{:S(2)}) %collective-permute-start.2) | collective-permute-done | bytes 6176 | tf_op jit(solution)/shard_map/while/body/eval_jaxpr/ppermute | solution.py:34
  98.8 2.4 collective-permute-start.1
  101.3 4.6 collective-permute-done.1
  107.2 5.7 %collective-permute-done.2 = f32[3,2,256]{2,1,0:T(2,128)S(1)} collective-permute-done((f32[3,2,256]{2,1,0:T(2,128)S(1)}, f32[3,2,256]{2,1,0:T(2,128)S(1)}, u32[]{:S(2)}, u32[]{:S(2)}) %collective-permute-start.2) | collective-permute-done | bytes 6176 | tf_op jit(solution)/shard_map/while/body/eval_jaxpr/ppermute | solution.py:34
  114.9 2.4 collective-permute-start.1
  117.3 4.6 collective-permute-done.1
  123.2 5.7 %collective-permute-done.2 = f32[3,2,256]{2,1,0:T(2,128)S(1)} collective-permute-done((f32[3,2,256]{2,1,0:T(2,128)S(1)}, f32[3,2,256]{2,1,0:T(2,128)S(1)}, u32[]{:S(2)}, u32[]{:S(2)}) %collective-permute-start.2) | collective-permute-done | bytes 6176 | tf_op jit(solution)/shard_map/while/body/eval_jaxpr/ppermute | solution.py:34
  133.3 4.6 collective-permute-done.1
  139.3 5.7 %collective-permute-done.2 = f32[3,2,256]{2,1,0:T(2,128)S(1)} collective-permute-done((f32[3,2,256]{2,1,0:T(2,128)S(1)}, f32[3,2,256]{2,1,0:T(2,128)S(1)}, u32[]{:S(2)}, u32[]{:S(2)}) %collective-permute-start.2) | collective-permute-done | bytes 6176 | tf_op jit(solution)/shard_map/while/body/eval_jaxpr/ppermute | solution.py:34
  149.4 4.6 collective-permute-done.1
  155.3 6.6 %collective-permute-done.2 = f32[3,2,256]{2,1,0:T(2,128)S(1)} collective-permute-done((f32[3,2,256]{2,1,0:T(2,128)S(1)}, f32[3,2,256]{2,1,0:T(2,128)S(1)}, u32[]{:S(2)}, u32[]{:S(2)}) %collective-permute-start.2) | collective-permute-done | bytes 6176 | tf_op jit(solution)/shard_map/while/body/eval_jaxpr/ppermute | solution.py:34
  166.3 4.6 collective-permute-done.1
  172.2 6.6 %collective-permute-done.2 = f32[3,2,256]{2,1,0:T(2,128)S(1)} collective-permute-done((f32[3,2,256]{2,1,0:T(2,128)S(1)}, f32[3,2,256]{2,1,0:T(2,128)S(1)}, u32[]{:S(2)}, u32[]{:S(2)}) %collective-permute-start.2) | collective-permute-done | bytes 6176 | tf_op jit(solution)/shard_map/while/body/eval_jaxpr/ppermute | solution.py:34
  183.2 4.6 collective-permute-done.1
  189.1 6.6 %collective-permute-done.2 = f32[3,2,256]{2,1,0:T(2,128)S(1)} collective-permute-done((f32[3,2,256]{2,1,0:T(2,128)S(1)}, f32[3,2,256]{2,1,0:T(2,128)S(1)}, u32[]{:S(2)}, u32[]{:S(2)}) %collective-permute-start.2) | collective-permute-done | bytes 6176 | tf_op jit(solution)/shard_map/while/body/eval_jaxpr/ppermute | solution.py:34
  200.1 4.6 collective-permute-done.1
  206.1 6.6 %collective-permute-done.2 = f32[3,2,256]{2,1,0:T(2,128)S(1)} collective-permute-done((f32[3,2,256]{2,1,0:T(2,128)S(1)}, f32[3,2,256]{2,1,0:T(2,128)S(1)}, u32[]{:S(2)}, u32[]{:S(2)}) %collective-permute-start.2) | collective-permute-done | bytes 6176 | tf_op jit(solution)/shard_map/while/body/eval_jaxpr/ppermute | solution.py:34
  217.1 4.6 collective-permute-done.1
  223.0 6.6 %collective-permute-done.2 = f32[3,2,256]{2,1,0:T(2,128)S(1)} collective-permute-done((f32[3,2,256]{2,1,0:T(2,128)S(1)}, f32[3,2,256]{2,1,0:T(2,128)S(1)}, u32[]{:S(2)}, u32[]{:S(2)}) %collective-permute-start.2) | collective-permute-done | bytes 6176 | tf_op jit(solution)/shard_map/while/body/eval_jaxpr/ppermute | solution.py:34
  234.0 4.6 collective-permute-done.1
  239.9 6.6 %collective-permute-done.2 = f32[3,2,256]{2,1,0:T(2,128)S(1)} collective-permute-done((f32[3,2,256]{2,1,0:T(2,128)S(1)}, f32[3,2,256]{2,1,0:T(2,128)S(1)}, u32[]{:S(2)}, u32[]{:S(2)}) %collective-permute-start.2) | collective-permute-done | bytes 6176 | tf_op jit(solution)/shard_map/while/body/eval_jaxpr/ppermute | solution.py:34
  250.9 4.6 collective-permute-done.1
  256.9 6.6 %collective-permute-done.2 = f32[3,2,256]{2,1,0:T(2,128)S(1)} collective-permute-done((f32[3,2,256]{2,1,0:T(2,128)S(1)}, f32[3,2,256]{2,1,0:T(2,128)S(1)}, u32[]{:S(2)}, u32[]{:S(2)}) %collective-permute-start.2) | collective-permute-done | bytes 6176 | tf_op jit(solution)/shard_map/while/body/eval_jaxpr/ppermute | solution.py:34
  267.9 4.6 collective-permute-done.1
  273.8 6.6 %collective-permute-done.2 = f32[3,2,256]{2,1,0:T(2,128)S(1)} collective-permute-done((f32[3,2,256]{2,1,0:T(2,128)S(1)}, f32[3,2,256]{2,1,0:T(2,128)S(1)}, u32[]{:S(2)}, u32[]{:S(2)}) %collective-permute-start.2) | collective-permute-done | bytes 6176 | tf_op jit(solution)/shard_map/while/body/eval_jaxpr/ppermute | solution.py:34
  284.8 4.6 collective-permute-done.1
  290.7 6.6 %collective-permute-done.2 = f32[3,2,256]{2,1,0:T(2,128)S(1)} collective-permute-done((f32[3,2,256]{2,1,0:T(2,128)S(1)}, f32[3,2,256]{2,1,0:T(2,128)S(1)}, u32[]{:S(2)}, u32[]{:S(2)}) %collective-permute-start.2) | collective-permute-done | bytes 6176 | tf_op jit(solution)/shard_map/while/body/eval_jaxpr/ppermute | solution.py:34
  301.7 4.6 collective-permute-done.1
  307.7 6.6 %collective-permute-done.2 = f32[3,2,256]{2,1,0:T(2,128)S(1)} collective-permute-done((f32[3,2,256]{2,1,0:T(2,128)S(1)}, f32[3,2,256]{2,1,0:T(2,128)S(1)}, u32[]{:S(2)}, u32[]{:S(2)}) %collective-permute-start.2) | collective-permute-done | bytes 6176 | tf_op jit(solution)/shard_map/while/body/eval_jaxpr/ppermute | solution.py:34
  318.7 4.6 collective-permute-done.1
  324.6 135.9 %collective-permute-done.2 = f32[3,2,256]{2,1,0:T(2,128)S(1)} collective-permute-done((f32[3,2,256]{2,1,0:T(2,128)S(1)}, f32[3,2,256]{2,1,0:T(2,128)S(1)}, u32[]{:S(2)}, u32[]{:S(2)}) %collective-permute-start.2) | collective-permute-done | bytes 6176 | tf_op jit(solution)/shard_map/while/body/eval_jaxpr/ppermute | solution.py:34
  464.9 4.6 collective-permute-done.1
  469.5 11.0 %conditional.2 = ((f32[3,2,256]{2,1,0:T(2,128)S(1)}, f32[3,2,256]{2,1,0:T(2,128)S(1)})) conditional(s32[]{:T(128)} %convert_element_type.30, (f32[3,2,256]{2,1,0:T(2,128)S(1)}, f32[3,2,256]{2,1,0:T(2,128)S(1)}) %tuple.105, (f32[256]{0:T(256)S(1)}, f32[256,3]{0,1:T(4,128)S(1)}, f32[3,4,256]{2,1,0:T(4,128)S(1)}, bf16[3,3,256,256]{3,2,1,0:T(8,128)(2,1)S(1)}, ...), branch_computations={%region_4.4_spmd, %region_5.5_spmd} | conditional | flops 614206464 | bytes 25134088 | solution.py:126
  481.9 5.7 %collective-permute-done.2 = f32[3,2,256]{2,1,0:T(2,128)S(1)} collective-permute-done((f32[3,2,256]{2,1,0:T(2,128)S(1)}, f32[3,2,256]{2,1,0:T(2,128)S(1)}, u32[]{:S(2)}, u32[]{:S(2)}) %collective-permute-start.2) | collective-permute-done | bytes 6176 | tf_op jit(solution)/shard_map/while/body/eval_jaxpr/ppermute | solution.py:34
  490.0 4.0 fusion.48
  494.0 3.0 copy.103
  (264 shorter events, 126.4 us)
Async XLA Ops:
  9.3 19.0 %collective-permute-start.11 = (f32[3,1,256]{2,1,0:T(1,128)S(1)}, f32[3,1,256]{2,1,0:T(1,128)S(1)}, u32[]{:S(2)}, u32[]{:S(2)}) collective-permute-start(f32[3,1,256]{2,1,0:T(1,128)S(1)} %get-tuple-element.321), channel_id=1, source_target_pairs={{0,1},{1,2},{2,3},{3,4},{4,5},{5,6},{6,7},{7,8},{8,9},{9,10},{10,1... | collective-permute-start | bytes 9224 | tf_op jit(solution)/shard_map/ppermute | solution.py:22
  11.2 17.1 %collective-permute-start.12 = (f32[3,1,256]{2,1,0:T(1,128)S(1)}, f32[3,1,256]{2,1,0:T(1,128)S(1)}, u32[]{:S(2)}, u32[]{:S(2)}) collective-permute-start(f32[3,1,256]{2,1,0:T(1,128)S(1)} %get-tuple-element.322), channel_id=1, source_target_pairs={{1,0},{2,1},{3,2},{4,3},{5,4},{6,5},{7,6},{8,7},{9,8},{10,9},{11,1... | collective-permute-start | bytes 9224 | tf_op jit(solution)/shard_map/ppermute | solution.py:24
  22.9 16.9 %collective-permute-start.3 = (f32[3,1,2048]{2,1,0:T(1,128)}, f32[3,1,2048]{2,1,0:T(1,128)}, u32[]{:S(2)}, u32[]{:S(2)}) collective-permute-start(f32[3,1,2048]{2,1,0:T(1,128)} %get-tuple-element.313), channel_id=1, source_target_pairs={{1,0},{2,1},{3,2},{4,3},{5,4},{6,5},{7,6},{8,7},{9,8},{10,9},{11,1... | collective-permute-start | bytes 73736 | tf_op jit(solution)/shard_map/ppermute | solution.py:24
  25.5 14.3 %collective-permute-start.4 = (f32[3,1,2048]{2,1,0:T(1,128)}, f32[3,1,2048]{2,1,0:T(1,128)}, u32[]{:S(2)}, u32[]{:S(2)}) collective-permute-start(f32[3,1,2048]{2,1,0:T(1,128)} %get-tuple-element.312), channel_id=1, source_target_pairs={{0,1},{1,2},{2,3},{3,4},{4,5},{5,6},{6,7},{7,8},{8,9},{9,10},{10,1... | collective-permute-start | bytes 73736 | tf_op jit(solution)/shard_map/ppermute | solution.py:22
  41.2 7.9 %collective-permute-start.5 = (f32[3,1,2048]{2,1,0:T(1,128)S(1)}, f32[3,1,2048]{2,1,0:T(1,128)S(1)}, u32[]{:S(2)}, u32[]{:S(2)}) collective-permute-start(f32[3,1,2048]{2,1,0:T(1,128)S(1)} %get-tuple-element.307), channel_id=1, source_target_pairs={{1,0},{2,1},{3,2},{4,3},{5,4},{6,5},{7,6},{8,7},{9,8},{10,9},{11,1... | collective-permute-start | bytes 73736 | tf_op jit(solution)/shard_map/ppermute | solution.py:24
  47.0 7.3 %collective-permute-start.6 = (f32[3,1,2048]{2,1,0:T(1,128)S(1)}, f32[3,1,2048]{2,1,0:T(1,128)S(1)}, u32[]{:S(2)}, u32[]{:S(2)}) collective-permute-start(f32[3,1,2048]{2,1,0:T(1,128)S(1)} %get-tuple-element.306), channel_id=1, source_target_pairs={{0,1},{1,2},{2,3},{3,4},{4,5},{5,6},{6,7},{7,8},{8,9},{9,10},{10,1... | collective-permute-start | bytes 73736 | tf_op jit(solution)/shard_map/ppermute | solution.py:22
  55.0 4.4 collective-permute-start.7
  56.9 7.3 %collective-permute-start.8 = (f32[3,1,2048]{2,1,0:T(1,128)S(1)}, f32[3,1,2048]{2,1,0:T(1,128)S(1)}, u32[]{:S(2)}, u32[]{:S(2)}) collective-permute-start(f32[3,1,2048]{2,1,0:T(1,128)S(1)} %get-tuple-element.300), channel_id=1, source_target_pairs={{0,1},{1,2},{2,3},{3,4},{4,5},{5,6},{6,7},{7,8},{8,9},{9,10},{10,1... | collective-permute-start | bytes 73736 | tf_op jit(solution)/shard_map/ppermute | solution.py:22
  64.9 7.8 %collective-permute-start.10 = (f32[3,1,2048]{2,1,0:T(1,128)S(1)}, f32[3,1,2048]{2,1,0:T(1,128)S(1)}, u32[]{:S(2)}, u32[]{:S(2)}) collective-permute-start(f32[3,1,2048]{2,1,0:T(1,128)S(1)} %get-tuple-element.294), channel_id=1, source_target_pairs={{0,1},{1,2},{2,3},{3,4},{4,5},{5,6},{6,7},{7,8},{8,9},{9,10},{10,1... | collective-permute-start | bytes 73736 | tf_op jit(solution)/shard_map/ppermute | solution.py:22
  66.9 7.3 %collective-permute-start.9 = (f32[3,1,2048]{2,1,0:T(1,128)S(1)}, f32[3,1,2048]{2,1,0:T(1,128)S(1)}, u32[]{:S(2)}, u32[]{:S(2)}) collective-permute-start(f32[3,1,2048]{2,1,0:T(1,128)S(1)} %get-tuple-element.295), channel_id=1, source_target_pairs={{1,0},{2,1},{3,2},{4,3},{5,4},{6,5},{7,6},{8,7},{9,8},{10,9},{11,1... | collective-permute-start | bytes 73736 | tf_op jit(solution)/shard_map/ppermute | solution.py:24
  77.0 7.7 %collective-permute-start = (f32[3,1,256]{2,1,0:T(1,128)S(1)}, f32[3,1,256]{2,1,0:T(1,128)S(1)}, u32[]{:S(2)}, u32[]{:S(2)}) collective-permute-start(f32[3,1,256]{2,1,0:T(1,128)S(1)} %get-tuple-element.397), channel_id=1, source_target_pairs={{1,0},{2,1},{3,2},{4,3},{5,4},{6,5},{7,6},{8,7},{9,8},{10,9},{11,1... | collective-permute-start | bytes 9224 | tf_op jit(solution)/shard_map/while/body/eval_jaxpr/ppermute | solution.py:24
  82.8 7.0 %collective-permute-start.1 = (f32[3,1,256]{2,1,0:T(1,128)S(1)}, f32[3,1,256]{2,1,0:T(1,128)S(1)}, u32[]{:S(2)}, u32[]{:S(2)}) collective-permute-start(f32[3,1,256]{2,1,0:T(1,128)S(1)} %get-tuple-element.398), channel_id=1, source_target_pairs={{0,1},{1,2},{2,3},{3,4},{4,5},{5,6},{6,7},{7,8},{8,9},{9,10},{10,1... | collective-permute-start | bytes 9224 | tf_op jit(solution)/shard_map/while/body/eval_jaxpr/ppermute | solution.py:22
  89.9 7.0 %collective-permute-start.2 = (f32[3,2,256]{2,1,0:T(2,128)S(1)}, f32[3,2,256]{2,1,0:T(2,128)S(1)}, u32[]{:S(2)}, u32[]{:S(2)}) collective-permute-start(f32[3,2,256]{2,1,0:T(2,128)S(1)} %get-tuple-element.399), channel_id=1, source_target_pairs={{0,32},{32,64},{64,96},{96,128},{128,160},{160,192},{192,224},{224... | collective-permute-start | bytes 18440 | tf_op jit(solution)/shard_map/while/body/eval_jaxpr/ppermute | solution.py:34
  98.8 7.0 %collective-permute-start.1 = (f32[3,1,256]{2,1,0:T(1,128)S(1)}, f32[3,1,256]{2,1,0:T(1,128)S(1)}, u32[]{:S(2)}, u32[]{:S(2)}) collective-permute-start(f32[3,1,256]{2,1,0:T(1,128)S(1)} %get-tuple-element.398), channel_id=1, source_target_pairs={{0,1},{1,2},{2,3},{3,4},{4,5},{5,6},{6,7},{7,8},{8,9},{9,10},{10,1... | collective-permute-start | bytes 9224 | tf_op jit(solution)/shard_map/while/body/eval_jaxpr/ppermute | solution.py:22
  105.9 7.0 %collective-permute-start.2 = (f32[3,2,256]{2,1,0:T(2,128)S(1)}, f32[3,2,256]{2,1,0:T(2,128)S(1)}, u32[]{:S(2)}, u32[]{:S(2)}) collective-permute-start(f32[3,2,256]{2,1,0:T(2,128)S(1)} %get-tuple-element.399), channel_id=1, source_target_pairs={{0,32},{32,64},{64,96},{96,128},{128,160},{160,192},{192,224},{224... | collective-permute-start | bytes 18440 | tf_op jit(solution)/shard_map/while/body/eval_jaxpr/ppermute | solution.py:34
  112.9 4.4 collective-permute-start
  114.9 7.0 %collective-permute-start.1 = (f32[3,1,256]{2,1,0:T(1,128)S(1)}, f32[3,1,256]{2,1,0:T(1,128)S(1)}, u32[]{:S(2)}, u32[]{:S(2)}) collective-permute-start(f32[3,1,256]{2,1,0:T(1,128)S(1)} %get-tuple-element.398), channel_id=1, source_target_pairs={{0,1},{1,2},{2,3},{3,4},{4,5},{5,6},{6,7},{7,8},{8,9},{9,10},{10,1... | collective-permute-start | bytes 9224 | tf_op jit(solution)/shard_map/while/body/eval_jaxpr/ppermute | solution.py:22
  121.9 7.0 %collective-permute-start.2 = (f32[3,2,256]{2,1,0:T(2,128)S(1)}, f32[3,2,256]{2,1,0:T(2,128)S(1)}, u32[]{:S(2)}, u32[]{:S(2)}) collective-permute-start(f32[3,2,256]{2,1,0:T(2,128)S(1)} %get-tuple-element.399), channel_id=1, source_target_pairs={{0,32},{32,64},{64,96},{96,128},{128,160},{160,192},{192,224},{224... | collective-permute-start | bytes 18440 | tf_op jit(solution)/shard_map/while/body/eval_jaxpr/ppermute | solution.py:34
  129.0 4.4 collective-permute-start
  130.9 7.0 %collective-permute-start.1 = (f32[3,1,256]{2,1,0:T(1,128)S(1)}, f32[3,1,256]{2,1,0:T(1,128)S(1)}, u32[]{:S(2)}, u32[]{:S(2)}) collective-permute-start(f32[3,1,256]{2,1,0:T(1,128)S(1)} %get-tuple-element.398), channel_id=1, source_target_pairs={{0,1},{1,2},{2,3},{3,4},{4,5},{5,6},{6,7},{7,8},{8,9},{9,10},{10,1... | collective-permute-start | bytes 9224 | tf_op jit(solution)/shard_map/while/body/eval_jaxpr/ppermute | solution.py:22
  138.0 7.0 %collective-permute-start.2 = (f32[3,2,256]{2,1,0:T(2,128)S(1)}, f32[3,2,256]{2,1,0:T(2,128)S(1)}, u32[]{:S(2)}, u32[]{:S(2)}) collective-permute-start(f32[3,2,256]{2,1,0:T(2,128)S(1)} %get-tuple-element.399), channel_id=1, source_target_pairs={{0,32},{32,64},{64,96},{96,128},{128,160},{160,192},{192,224},{224... | collective-permute-start | bytes 18440 | tf_op jit(solution)/shard_map/while/body/eval_jaxpr/ppermute | solution.py:34
  145.0 4.4 collective-permute-start
  146.9 7.0 %collective-permute-start.1 = (f32[3,1,256]{2,1,0:T(1,128)S(1)}, f32[3,1,256]{2,1,0:T(1,128)S(1)}, u32[]{:S(2)}, u32[]{:S(2)}) collective-permute-start(f32[3,1,256]{2,1,0:T(1,128)S(1)} %get-tuple-element.398), channel_id=1, source_target_pairs={{0,1},{1,2},{2,3},{3,4},{4,5},{5,6},{6,7},{7,8},{8,9},{9,10},{10,1... | collective-permute-start | bytes 9224 | tf_op jit(solution)/shard_map/while/body/eval_jaxpr/ppermute | solution.py:22
  154.0 7.9 %collective-permute-start.2 = (f32[3,2,256]{2,1,0:T(2,128)S(1)}, f32[3,2,256]{2,1,0:T(2,128)S(1)}, u32[]{:S(2)}, u32[]{:S(2)}) collective-permute-start(f32[3,2,256]{2,1,0:T(2,128)S(1)} %get-tuple-element.399), channel_id=1, source_target_pairs={{0,32},{32,64},{64,96},{96,128},{128,160},{160,192},{192,224},{224... | collective-permute-start | bytes 18440 | tf_op jit(solution)/shard_map/while/body/eval_jaxpr/ppermute | solution.py:34
  163.8 7.0 %collective-permute-start.1 = (f32[3,1,256]{2,1,0:T(1,128)S(1)}, f32[3,1,256]{2,1,0:T(1,128)S(1)}, u32[]{:S(2)}, u32[]{:S(2)}) collective-permute-start(f32[3,1,256]{2,1,0:T(1,128)S(1)} %get-tuple-element.398), channel_id=1, source_target_pairs={{0,1},{1,2},{2,3},{3,4},{4,5},{5,6},{6,7},{7,8},{8,9},{9,10},{10,1... | collective-permute-start | bytes 9224 | tf_op jit(solution)/shard_map/while/body/eval_jaxpr/ppermute | solution.py:22
  170.9 7.9 %collective-permute-start.2 = (f32[3,2,256]{2,1,0:T(2,128)S(1)}, f32[3,2,256]{2,1,0:T(2,128)S(1)}, u32[]{:S(2)}, u32[]{:S(2)}) collective-permute-start(f32[3,2,256]{2,1,0:T(2,128)S(1)} %get-tuple-element.399), channel_id=1, source_target_pairs={{0,32},{32,64},{64,96},{96,128},{128,160},{160,192},{192,224},{224... | collective-permute-start | bytes 18440 | tf_op jit(solution)/shard_map/while/body/eval_jaxpr/ppermute | solution.py:34
  178.9 4.4 collective-permute-start
  180.8 7.0 %collective-permute-start.1 = (f32[3,1,256]{2,1,0:T(1,128)S(1)}, f32[3,1,256]{2,1,0:T(1,128)S(1)}, u32[]{:S(2)}, u32[]{:S(2)}) collective-permute-start(f32[3,1,256]{2,1,0:T(1,128)S(1)} %get-tuple-element.398), channel_id=1, source_target_pairs={{0,1},{1,2},{2,3},{3,4},{4,5},{5,6},{6,7},{7,8},{8,9},{9,10},{10,1... | collective-permute-start | bytes 9224 | tf_op jit(solution)/shard_map/while/body/eval_jaxpr/ppermute | solution.py:22
  187.8 7.9 %collective-permute-start.2 = (f32[3,2,256]{2,1,0:T(2,128)S(1)}, f32[3,2,256]{2,1,0:T(2,128)S(1)}, u32[]{:S(2)}, u32[]{:S(2)}) collective-permute-start(f32[3,2,256]{2,1,0:T(2,128)S(1)} %get-tuple-element.399), channel_id=1, source_target_pairs={{0,32},{32,64},{64,96},{96,128},{128,160},{160,192},{192,224},{224... | collective-permute-start | bytes 18440 | tf_op jit(solution)/shard_map/while/body/eval_jaxpr/ppermute | solution.py:34
  195.8 4.4 collective-permute-start
  197.7 7.0 %collective-permute-start.1 = (f32[3,1,256]{2,1,0:T(1,128)S(1)}, f32[3,1,256]{2,1,0:T(1,128)S(1)}, u32[]{:S(2)}, u32[]{:S(2)}) collective-permute-start(f32[3,1,256]{2,1,0:T(1,128)S(1)} %get-tuple-element.398), channel_id=1, source_target_pairs={{0,1},{1,2},{2,3},{3,4},{4,5},{5,6},{6,7},{7,8},{8,9},{9,10},{10,1... | collective-permute-start | bytes 9224 | tf_op jit(solution)/shard_map/while/body/eval_jaxpr/ppermute | solution.py:22
  204.8 7.9 %collective-permute-start.2 = (f32[3,2,256]{2,1,0:T(2,128)S(1)}, f32[3,2,256]{2,1,0:T(2,128)S(1)}, u32[]{:S(2)}, u32[]{:S(2)}) collective-permute-start(f32[3,2,256]{2,1,0:T(2,128)S(1)} %get-tuple-element.399), channel_id=1, source_target_pairs={{0,32},{32,64},{64,96},{96,128},{128,160},{160,192},{192,224},{224... | collective-permute-start | bytes 18440 | tf_op jit(solution)/shard_map/while/body/eval_jaxpr/ppermute | solution.py:34
  214.6 7.0 %collective-permute-start.1 = (f32[3,1,256]{2,1,0:T(1,128)S(1)}, f32[3,1,256]{2,1,0:T(1,128)S(1)}, u32[]{:S(2)}, u32[]{:S(2)}) collective-permute-start(f32[3,1,256]{2,1,0:T(1,128)S(1)} %get-tuple-element.398), channel_id=1, source_target_pairs={{0,1},{1,2},{2,3},{3,4},{4,5},{5,6},{6,7},{7,8},{8,9},{9,10},{10,1... | collective-permute-start | bytes 9224 | tf_op jit(solution)/shard_map/while/body/eval_jaxpr/ppermute | solution.py:22
  221.7 7.9 %collective-permute-start.2 = (f32[3,2,256]{2,1,0:T(2,128)S(1)}, f32[3,2,256]{2,1,0:T(2,128)S(1)}, u32[]{:S(2)}, u32[]{:S(2)}) collective-permute-start(f32[3,2,256]{2,1,0:T(2,128)S(1)} %get-tuple-element.399), channel_id=1, source_target_pairs={{0,32},{32,64},{64,96},{96,128},{128,160},{160,192},{192,224},{224... | collective-permute-start | bytes 18440 | tf_op jit(solution)/shard_map/while/body/eval_jaxpr/ppermute | solution.py:34
  231.6 7.0 %collective-permute-start.1 = (f32[3,1,256]{2,1,0:T(1,128)S(1)}, f32[3,1,256]{2,1,0:T(1,128)S(1)}, u32[]{:S(2)}, u32[]{:S(2)}) collective-permute-start(f32[3,1,256]{2,1,0:T(1,128)S(1)} %get-tuple-element.398), channel_id=1, source_target_pairs={{0,1},{1,2},{2,3},{3,4},{4,5},{5,6},{6,7},{7,8},{8,9},{9,10},{10,1... | collective-permute-start | bytes 9224 | tf_op jit(solution)/shard_map/while/body/eval_jaxpr/ppermute | solution.py:22
  238.6 7.9 %collective-permute-start.2 = (f32[3,2,256]{2,1,0:T(2,128)S(1)}, f32[3,2,256]{2,1,0:T(2,128)S(1)}, u32[]{:S(2)}, u32[]{:S(2)}) collective-permute-start(f32[3,2,256]{2,1,0:T(2,128)S(1)} %get-tuple-element.399), channel_id=1, source_target_pairs={{0,32},{32,64},{64,96},{96,128},{128,160},{160,192},{192,224},{224... | collective-permute-start | bytes 18440 | tf_op jit(solution)/shard_map/while/body/eval_jaxpr/ppermute | solution.py:34
  248.5 7.0 %collective-permute-start.1 = (f32[3,1,256]{2,1,0:T(1,128)S(1)}, f32[3,1,256]{2,1,0:T(1,128)S(1)}, u32[]{:S(2)}, u32[]{:S(2)}) collective-permute-start(f32[3,1,256]{2,1,0:T(1,128)S(1)} %get-tuple-element.398), channel_id=1, source_target_pairs={{0,1},{1,2},{2,3},{3,4},{4,5},{5,6},{6,7},{7,8},{8,9},{9,10},{10,1... | collective-permute-start | bytes 9224 | tf_op jit(solution)/shard_map/while/body/eval_jaxpr/ppermute | solution.py:22
  255.6 7.9 %collective-permute-start.2 = (f32[3,2,256]{2,1,0:T(2,128)S(1)}, f32[3,2,256]{2,1,0:T(2,128)S(1)}, u32[]{:S(2)}, u32[]{:S(2)}) collective-permute-start(f32[3,2,256]{2,1,0:T(2,128)S(1)} %get-tuple-element.399), channel_id=1, source_target_pairs={{0,32},{32,64},{64,96},{96,128},{128,160},{160,192},{192,224},{224... | collective-permute-start | bytes 18440 | tf_op jit(solution)/shard_map/while/body/eval_jaxpr/ppermute | solution.py:34
  265.4 7.0 %collective-permute-start.1 = (f32[3,1,256]{2,1,0:T(1,128)S(1)}, f32[3,1,256]{2,1,0:T(1,128)S(1)}, u32[]{:S(2)}, u32[]{:S(2)}) collective-permute-start(f32[3,1,256]{2,1,0:T(1,128)S(1)} %get-tuple-element.398), channel_id=1, source_target_pairs={{0,1},{1,2},{2,3},{3,4},{4,5},{5,6},{6,7},{7,8},{8,9},{9,10},{10,1... | collective-permute-start | bytes 9224 | tf_op jit(solution)/shard_map/while/body/eval_jaxpr/ppermute | solution.py:22
  272.5 7.9 %collective-permute-start.2 = (f32[3,2,256]{2,1,0:T(2,128)S(1)}, f32[3,2,256]{2,1,0:T(2,128)S(1)}, u32[]{:S(2)}, u32[]{:S(2)}) collective-permute-start(f32[3,2,256]{2,1,0:T(2,128)S(1)} %get-tuple-element.399), channel_id=1, source_target_pairs={{0,32},{32,64},{64,96},{96,128},{128,160},{160,192},{192,224},{224... | collective-permute-start | bytes 18440 | tf_op jit(solution)/shard_map/while/body/eval_jaxpr/ppermute | solution.py:34
  282.4 7.0 %collective-permute-start.1 = (f32[3,1,256]{2,1,0:T(1,128)S(1)}, f32[3,1,256]{2,1,0:T(1,128)S(1)}, u32[]{:S(2)}, u32[]{:S(2)}) collective-permute-start(f32[3,1,256]{2,1,0:T(1,128)S(1)} %get-tuple-element.398), channel_id=1, source_target_pairs={{0,1},{1,2},{2,3},{3,4},{4,5},{5,6},{6,7},{7,8},{8,9},{9,10},{10,1... | collective-permute-start | bytes 9224 | tf_op jit(solution)/shard_map/while/body/eval_jaxpr/ppermute | solution.py:22
  289.4 7.9 %collective-permute-start.2 = (f32[3,2,256]{2,1,0:T(2,128)S(1)}, f32[3,2,256]{2,1,0:T(2,128)S(1)}, u32[]{:S(2)}, u32[]{:S(2)}) collective-permute-start(f32[3,2,256]{2,1,0:T(2,128)S(1)} %get-tuple-element.399), channel_id=1, source_target_pairs={{0,32},{32,64},{64,96},{96,128},{128,160},{160,192},{192,224},{224... | collective-permute-start | bytes 18440 | tf_op jit(solution)/shard_map/while/body/eval_jaxpr/ppermute | solution.py:34
  299.3 7.0 %collective-permute-start.1 = (f32[3,1,256]{2,1,0:T(1,128)S(1)}, f32[3,1,256]{2,1,0:T(1,128)S(1)}, u32[]{:S(2)}, u32[]{:S(2)}) collective-permute-start(f32[3,1,256]{2,1,0:T(1,128)S(1)} %get-tuple-element.398), channel_id=1, source_target_pairs={{0,1},{1,2},{2,3},{3,4},{4,5},{5,6},{6,7},{7,8},{8,9},{9,10},{10,1... | collective-permute-start | bytes 9224 | tf_op jit(solution)/shard_map/while/body/eval_jaxpr/ppermute | solution.py:22
  306.4 7.9 %collective-permute-start.2 = (f32[3,2,256]{2,1,0:T(2,128)S(1)}, f32[3,2,256]{2,1,0:T(2,128)S(1)}, u32[]{:S(2)}, u32[]{:S(2)}) collective-permute-start(f32[3,2,256]{2,1,0:T(2,128)S(1)} %get-tuple-element.399), channel_id=1, source_target_pairs={{0,32},{32,64},{64,96},{96,128},{128,160},{160,192},{192,224},{224... | collective-permute-start | bytes 18440 | tf_op jit(solution)/shard_map/while/body/eval_jaxpr/ppermute | solution.py:34
  316.2 7.0 %collective-permute-start.1 = (f32[3,1,256]{2,1,0:T(1,128)S(1)}, f32[3,1,256]{2,1,0:T(1,128)S(1)}, u32[]{:S(2)}, u32[]{:S(2)}) collective-permute-start(f32[3,1,256]{2,1,0:T(1,128)S(1)} %get-tuple-element.398), channel_id=1, source_target_pairs={{0,1},{1,2},{2,3},{3,4},{4,5},{5,6},{6,7},{7,8},{8,9},{9,10},{10,1... | collective-permute-start | bytes 9224 | tf_op jit(solution)/shard_map/while/body/eval_jaxpr/ppermute | solution.py:22
  323.3 137.2 %collective-permute-start.2 = (f32[3,2,256]{2,1,0:T(2,128)S(1)}, f32[3,2,256]{2,1,0:T(2,128)S(1)}, u32[]{:S(2)}, u32[]{:S(2)}) collective-permute-start(f32[3,2,256]{2,1,0:T(2,128)S(1)} %get-tuple-element.399), channel_id=1, source_target_pairs={{0,32},{32,64},{64,96},{96,128},{128,160},{160,192},{192,224},{224... | collective-permute-start | bytes 18440 | tf_op jit(solution)/shard_map/while/body/eval_jaxpr/ppermute | solution.py:34
  462.5 7.0 %collective-permute-start.1 = (f32[3,1,256]{2,1,0:T(1,128)S(1)}, f32[3,1,256]{2,1,0:T(1,128)S(1)}, u32[]{:S(2)}, u32[]{:S(2)}) collective-permute-start(f32[3,1,256]{2,1,0:T(1,128)S(1)} %get-tuple-element.398), channel_id=1, source_target_pairs={{0,1},{1,2},{2,3},{3,4},{4,5},{5,6},{6,7},{7,8},{8,9},{9,10},{10,1... | collective-permute-start | bytes 9224 | tf_op jit(solution)/shard_map/while/body/eval_jaxpr/ppermute | solution.py:22
  480.6 7.0 %collective-permute-start.2 = (f32[3,2,256]{2,1,0:T(2,128)S(1)}, f32[3,2,256]{2,1,0:T(2,128)S(1)}, u32[]{:S(2)}, u32[]{:S(2)}) collective-permute-start(f32[3,2,256]{2,1,0:T(2,128)S(1)} %get-tuple-element.399), channel_id=1, source_target_pairs={{0,32},{32,64},{64,96},{96,128},{128,160},{160,192},{192,224},{224... | collective-permute-start | bytes 18440 | tf_op jit(solution)/shard_map/while/body/eval_jaxpr/ppermute | solution.py:34
  (22 other events, 121.1 us)
where the time goes:
time: 499 us; the launch traced here: 497 us
  waiting for transfers between devices  316 us (63%)
  starting transfers between devices  131 us (26%)
  local copies, waits for them, and re-layouts  23 us (5%)
  other arithmetic  20.1 us (4%)
  matrix products  5.29 us (1%)
    ppermute x16, waiting for transfers between devices, passed_along(): lax.ppermute(value, axis, [(source, source + steps) for source in range(i...  231 us
    ppermute x21, waiting for transfers between devices, padded(): lax.ppermute(tail, axis, [(i, (i + 1) % count) for i in range(count)])  83.8 us
    ppermute x21, starting transfers between devices, padded(): lax.ppermute(head, axis, [((i + 1) % count, i) for i in range(count)])  61.6 us
    ppermute x21, starting transfers between devices, padded(): lax.ppermute(tail, axis, [(i, (i + 1) % count) for i in range(count)])  48.3 us
    ppermute x16, starting transfers between devices, passed_along(): lax.ppermute(value, axis, [(source, source + steps) for source in range(i...  20.7 us
  transfers between devices with their start and end apart: 58, of which 35 were waited for; matrix products, arithmetic and copies ran while one was open for 3% of the time, Pallas kernels for 0%

commit v1 on v0

v1 whole, which is shorter than its diff:
```python
import functools
import jax, jax.numpy as jnp
from jax import lax
from jax.experimental import pallas as pl
from jax.experimental.pallas import tpu as pltpu
from jax.sharding import PartitionSpec as P

f32, bf16 = jnp.float32, jnp.bfloat16
FINE = 4
RF = 8
time_step = 0.2
viscosity = 1.0
sound_sq = 1.0
N = 16
ROWS = 32
W1, W2 = 48, 32

def gelu(x):
    u = x * (0.7978845608028654 + 0.035677408136300125 * (x * x))
    h = 0.5 * x
    return h + h * jnp.tanh(u)

def lift_operand(s, lane):
    hi = s.astype(bf16)
    lo = (s - hi.astype(f32)).astype(bf16)
    one = jnp.ones_like(hi)
    return jnp.concatenate([jnp.where(lane < 64, hi, lo), jnp.where(lane < 64, hi, one)], axis=1)

def shifted(h, axis_size):
    return pltpu.roll(h, 1, 0), pltpu.roll(h, axis_size - 1, 0)

def chain_kernel(CR_L, CR_C, r_ref, wt_ref, lw_ref, ow_ref, cb_ref, out_ref, d_ref, s_ref, h_ref, lwm_ref, owm_ref):
    acc = r_ref[0]
    d_ref[0:4] = jnp.zeros((4, ROWS * W1), f32)
    d_ref[4:8] = acc
    for n in range(1, N - 1):
        acc = acc + r_ref[n]
        d_ref[4 * n + 4:4 * n + 8] = acc
    for q in range(ROWS * W1 // 128):
        t = d_ref[:, q * 128:(q + 1) * 128].T
        s_ref[q * 128:(q + 1) * 128, :] = jnp.concatenate([t, t], axis=1)
    krow = lax.broadcasted_iota(jnp.int32, (256, 256), 0)
    kslot = (krow & 63) >> 2
    ocol = (lax.broadcasted_iota(jnp.int32, (256, 128), 1) & 63) >> 2

    def step(m, k, pitch):
        off = (W1 - pitch) // 2
        lwm_ref[...] = jnp.where((kslot == m) | (krow >= 192), lw_ref[...].astype(f32), 0.0).astype(bf16)
        owm_ref[...] = jnp.where(ocol >= m, ow_ref[...].astype(f32), 0.0).astype(bf16)
        r_lo, r_hi = 14 - k, 18 + k

        def lift(row, n):
            cells = n * pitch
            if pitch == W1:
                s = s_ref[pl.ds(pl.multiple_of(row * W1, 16), cells), :]
            else:
                s = jnp.concatenate([s_ref[pl.ds(pl.multiple_of((row + i) * W1 + off, 8), pitch), :] for i in range(n)], axis=0)
            lane = lax.broadcasted_iota(jnp.int32, s.shape, 1)
            x = lift_operand(s, lane)
            h = gelu(jnp.dot(x, lwm_ref[...], preferred_element_type=f32))
            left, right = shifted(h, cells)
            dst = pl.ds(pl.multiple_of(row * pitch, 16), cells)
            h_ref[dst, 0:256] = left.astype(bf16)
            h_ref[dst, 256:512] = h.astype(bf16)
            h_ref[dst, 512:768] = right.astype(bf16)

        def conv(row, n):
            cells = n * pitch
            acc = None
            for di in range(3):
                src = pl.ds(pl.multiple_of((row + di - 1) * pitch, 16), cells)
                p = jnp.dot(h_ref[src, :], wt_ref[di], preferred_element_type=f32)
                acc = p if acc is None else acc + p
            act = gelu(acc + cb_ref[...]).astype(bf16)
            inc = jnp.dot(act, owm_ref[...], preferred_element_type=f32)
            if pitch == W1:
                dst = pl.ds(pl.multiple_of(row * W1, 16), cells)
                s_ref[dst, :] = s_ref[dst, :] + inc
            else:
                for i in range(n):
                    dst = pl.ds(pl.multiple_of((row + i) * W1 + off, 8), pitch)
                    s_ref[dst, :] = s_ref[dst, :] + inc[i * pitch:(i + 1) * pitch]

        def sweep(body, lo, hi, chunk):
            full = (hi - lo) // chunk
            if full > 1:
                lax.fori_loop(0, full, lambda i, c: (body(lo + i * chunk, chunk), c)[1], 0)
            elif full == 1:
                body(lo, chunk)
            rest = (hi - lo) % chunk
            if rest:
                body(lo + full * chunk, rest)

        sweep(lift, r_lo, r_hi, CR_L)
        sweep(conv, r_lo + 1, r_hi - 1, CR_C)

    for m in range(1, N):
        k = N - 1 - m
        step(m, k, W1 if k > 7 else W2)
    g = jnp.concatenate([s_ref[15 * W1 + 16:15 * W1 + 32, :], s_ref[16 * W1 + 16:16 * W1 + 32, :]], axis=0)
    gt = g.T
    for n in range(N):
        out_ref[n] = gt[4 * n:4 * n + 4, :]

def chain(recv, wt, lw, ow, cb, CR_L=8, CR_C=8):
    L = ROWS * W1
    vm = pl.BlockSpec(memory_space=pltpu.VMEM)
    return pl.pallas_call(
        functools.partial(chain_kernel, CR_L, CR_C),
        out_shape=jax.ShapeDtypeStruct((N, 4, 32), f32),
        in_specs=[vm] * 5, out_specs=vm,
        scratch_shapes=[pltpu.VMEM((64, L), f32), pltpu.VMEM((L, 128), f32), pltpu.VMEM((L, 768), bf16),
                        pltpu.VMEM((256, 256), bf16), pltpu.VMEM((256, 128), bf16)],
        compiler_params=pltpu.CompilerParams(vmem_limit_bytes=48 * 2**20),
    )(recv, wt, lw, ow, cb)

def tables(lift_weight, lift_bias, conv_weight, conv_bias, out_weight):
    wt = conv_weight.transpose(0, 1, 3, 2).reshape(3, 768, 256)
    w4 = jnp.concatenate([lift_weight.T, jnp.zeros((1, 256), f32)], 0)
    hi = w4.astype(bf16); lo = (w4 - hi.astype(f32)).astype(bf16)
    bh = lift_bias.astype(bf16); bl = (lift_bias - bh.astype(f32)).astype(bf16)
    lw = jnp.concatenate([jnp.tile(hi, (32, 1)), jnp.tile(lo, (16, 1)), bh[None], bl[None], jnp.zeros((62, 256), bf16)], 0)
    ow = jnp.tile(jnp.concatenate([out_weight, jnp.zeros((1, 256), bf16)], 0), (32, 1)).T
    return wt, lw, ow, conv_bias[None]

def thirds(x):
    hi = x.astype(bf16)
    rest = x - hi.astype(f32)
    mid = rest.astype(bf16)
    low = (rest - mid.astype(f32)).astype(bf16)
    return jnp.concatenate([hi, mid, low], axis=0)

def exact_dot(x, pattern):
    n = x.shape[0]
    y = jnp.dot(thirds(x), pattern, preferred_element_type=f32)
    return y[0:n] + y[n:2 * n] + y[2 * n:3 * n]

def fine_step(a, b, q):
    def parts(x):
        e, w = pltpu.roll(x, x.shape[1] - 1, 1), pltpu.roll(x, 1, 1)
        n, s = pltpu.roll(x, 1, 0), pltpu.roll(x, x.shape[0] - 1, 0)
        return e - w, s - n, (e + w) + (n + s)
    ax, ay, al = parts(a)
    bx, by, bl = parts(b)
    qx, qy, ql = parts(q)
    half, keep = 0.5 * time_step, 1.0 - 4.0 * time_step * viscosity
    new_a = keep * a + time_step * viscosity * al - half * (a * ax + b * ay + qx)
    new_b = keep * b + time_step * viscosity * bl - half * (a * bx + b * by + qy)
    new_q = keep * q + time_step * viscosity * ql - half * sound_sq * (ax + by)
    return new_a, new_b, new_q

def first_kernel(tm_ref, s_ref, up_ref, dn_ref, wt_ref, lw_ref, ow_ref, cb_ref, corr_ref, c_ref, q_ref, h_ref):
    fields = [jnp.concatenate([up_ref[f], s_ref[0, f], dn_ref[f]], axis=0) for f in range(3)]
    q_ref[...] = jnp.zeros(q_ref.shape, f32)
    for f in range(3):
        for r in range(4):
            q_ref[4 * r + f:4 * r + f + 1, :] = jnp.sum(fields[f][8 * r:8 * r + 8], axis=0, keepdims=True)
    for _ in range(FINE):
        fields = fine_step(*fields)
    for f in range(3):
        for r in range(2):
            q_ref[16 + 4 * r + f:17 + 4 * r + f, :] = jnp.sum(fields[f][8 + 8 * r:16 + 8 * r], axis=0, keepdims=True)
    half = 128 * RF
    pool = (lax.broadcasted_iota(jnp.int32, (half, 128), 0) // RF == lax.broadcasted_iota(jnp.int32, (half, 128), 1)).astype(f32).astype(bf16)
    spread = (lax.broadcasted_iota(jnp.int32, (128, half), 1) // RF == lax.broadcasted_iota(jnp.int32, (128, half), 0)).astype(f32).astype(bf16)
    pooled = jnp.concatenate([exact_dot(q_ref[:, 0:half], pool), exact_dot(q_ref[:, half:], pool)], axis=1) * (1.0 / (RF * RF))
    pad = jnp.zeros((48, 256), f32)
    s = jnp.concatenate([pooled[0:16], pad, pooled[0:16], pad], axis=0).T
    x = lift_operand(s, lax.broadcasted_iota(jnp.int32, s.shape, 1))
    krow = lax.broadcasted_iota(jnp.int32, (256, 256), 0)
    kslot = (krow & 63) >> 2
    lw = lw_ref[...].astype(f32)
    for r in range(4):
        lwm = jnp.where((kslot == r) | (krow >= 192), lw, 0.0).astype(bf16)
        h = gelu(jnp.dot(x, lwm, preferred_element_type=f32))
        left, right = shifted(h, 256)
        h_ref[256 * r:256 * r + 256, 0:256] = left.astype(bf16)
        h_ref[256 * r:256 * r + 256, 256:512] = h.astype(bf16)
        h_ref[256 * r:256 * r + 256, 512:768] = right.astype(bf16)
    acc = jnp.dot(h_ref[0:512], wt_ref[0], preferred_element_type=f32)
    acc = acc + jnp.dot(h_ref[256:768], wt_ref[1], preferred_element_type=f32)
    acc = acc + jnp.dot(h_ref[512:1024], wt_ref[2], preferred_element_type=f32)
    act = gelu(acc + cb_ref[...]).astype(bf16)
    inc = jnp.dot(act, ow_ref[...], preferred_element_type=f32)
    lane = lax.broadcasted_iota(jnp.int32, s.shape, 1)
    guess = (s + jnp.where(lane < 8, inc[0:256], inc[256:512])).T[4:12]
    first = jnp.where(tm_ref[0] == 0, guess, 0.0)
    c = first + (pooled[16:24] - guess)
    for i in range(c_ref.shape[0]):
        c_ref[i] = c
    delta = guess - first
    for p in range(2):
        wide = exact_dot(delta[:, 128 * p:128 * p + 128], spread)
        for f in range(3):
            for r in range(2):
                corr_ref[f, 8 * r:8 * r + 8, half * p:half * p + half] = fields[f][8 + 8 * r:16 + 8 * r, half * p:half * p + half] - wide[4 * r + f:4 * r + f + 1]

def window_kernel(sp_ref, b_ref, out_ref):
    count = b_ref.shape[0]
    for q in range(ROWS):
        dev = lax.rem(sp_ref[0] + (count - 8 + (q + 1) // 2), count)
        r = (q + 1) % 2
        v = b_ref[dev, 4 * r:4 * r + 4, :]
        ext = jnp.concatenate([v[:, 240:256], v, v[:, 0:16]], axis=1)
        for j in range(N):
            out_ref[j, :, q * W1:(q + 1) * W1] = ext[:, 16 * j:16 * j + W1]

def last_kernel(g_ref, corr_ref, out_ref, y_ref):
    for j in range(N):
        y_ref[4 * j:4 * j + 4, :] = g_ref[j]
    row = lax.broadcasted_iota(jnp.int32, (32, 128), 0)
    col = lax.broadcasted_iota(jnp.int32, (32, 128), 1)
    for r in range(2):
        pattern = (row - 16 * r == col // RF).astype(f32).astype(bf16)
        y = exact_dot(y_ref[...], pattern)
        for j in range(N):
            for f in range(3):
                out_ref[0, f, 8 * r:8 * r + 8, 128 * j:128 * j + 128] = corr_ref[f, 8 * r:8 * r + 8, 128 * j:128 * j + 128] + y[4 * j + f:4 * j + f + 1]

def shards(start_states, lift_weight, lift_bias, conv_weight, conv_bias, out_weight):
    vm = pl.BlockSpec(memory_space=pltpu.VMEM)
    sm = pl.BlockSpec(memory_space=pltpu.SMEM)
    params = pltpu.CompilerParams(vmem_limit_bytes=48 * 2**20)
    count = lax.axis_size("space")
    slab = start_states[0]
    up = lax.ppermute(slab[:, 8:], "space", [(i, (i + 1) % count) for i in range(count)])
    down = lax.ppermute(slab[:, :8], "space", [((i + 1) % count, i) for i in range(count)])
    weights = tables(lift_weight, lift_bias, conv_weight, conv_bias, out_weight)
    tm = lax.axis_index("tm").astype(jnp.int32).reshape(1)
    sp = lax.axis_index("space").astype(jnp.int32).reshape(1)
    corr, c = pl.pallas_call(
        first_kernel,
        out_shape=[jax.ShapeDtypeStruct(slab.shape, f32), jax.ShapeDtypeStruct((count, 8, 256), f32)],
        in_specs=[sm] + [vm] * 7, out_specs=[vm, vm],
        scratch_shapes=[pltpu.VMEM((24, slab.shape[2]), f32), pltpu.VMEM((1024, 768), bf16)],
        compiler_params=params, name="fine_and_guess",
    )(tm, start_states, up, down, *weights)
    c = lax.all_to_all(c, "space", 0, 0)
    send = pl.pallas_call(
        window_kernel, out_shape=jax.ShapeDtypeStruct((N, 4, ROWS * W1), f32),
        in_specs=[sm, vm], out_specs=vm, compiler_params=params, name="windows",
    )(sp, c)
    recv = lax.all_to_all(send, "tm", 0, 0)
    g = chain(recv, *weights)
    g = lax.all_to_all(g, "tm", 0, 0)
    return pl.pallas_call(
        last_kernel, out_shape=jax.ShapeDtypeStruct(start_states.shape, f32),
        in_specs=[vm, vm], out_specs=vm, scratch_shapes=[pltpu.VMEM((64, 32), f32)],
        compiler_params=params, name="correct",
    )(g, corr)

def solution(mesh):
    return jax.shard_map(
        shards, mesh=mesh,
        in_specs=(P("tm", None, "space", None), P(), P(), P(), P(), P()),
        out_specs=P("tm", None, "space", None), check_vma=False,
    )
```

time: 499 us -> 122 us (0.24)
  the two profiles are of different devices: /device:TPU:60 before, /device:TPU:2 now
where the time goes in v1:
time: 122 us; the launch traced here: 121 us
  Pallas kernels  46.3 us (38%)
  blocking collectives  37.1 us (30%)
  starting transfers between devices  18.8 us (15%)
  waiting for transfers between devices  12.1 us (10%)
  local copies, waits for them, and re-layouts  4.55 us (4%)
  other arithmetic  2.12 us (2%)
    pallas_call x1, Pallas kernels, chain(): pl.pallas_call(functools.partial(chain_kernel, CR_L, CR_C), out_shape=jax...  38.2 us
    all_to_all x1, blocking collectives, shards(): recv = lax.all_to_all(send, 'tm', 0, 0)  24.4 us
    all_to_all x1, starting transfers between devices, shards(): c = lax.all_to_all(c, 'space', 0, 0)  13.2 us
    all_to_all x1, blocking collectives, shards(): g = lax.all_to_all(g, 'tm', 0, 0)  12.7 us
    all_to_all x1, waiting for transfers between devices, shards(): c = lax.all_to_all(c, 'space', 0, 0)  12.1 us
    pallas_call x1, Pallas kernels, shards(): pl.pallas_call(first_kernel, out_shape=[jax.ShapeDtypeStruct(slab.shape,...  4.86 us
    ppermute x1, starting transfers between devices, shards(): lax.ppermute(slab[:, :8], 'space', [((i + 1) % count, i) for i in range(c...  3.64 us
  transfers between devices with their start and end apart: 3, of which 1 were waited for; matrix products, arithmetic and copies ran while one was open for 4% of the time, Pallas kernels for 0%

profile of v1, /device:TPU:2, one launch (start us, length us, event | category | flops | bytes accessed | tf_op | source)
XLA Modules:
  0.0 121.1 jit_solution(6995264060947398568)
XLA Ops:
  0.0 1.0 fusion
  1.1 1.9 %collective-permute-start = (f32[3,8,2048]{2,1,0:T(8,128)S(1)}, f32[3,8,2048]{2,1,0:T(8,128)S(1)}, u32[]{:S(2)}, u32[]{:S(2)}) collective-permute-start(f32[3,8,2048]{2,1,0:T(8,128)S(1)} %get-tuple-element.12), channel_id=1, source_target_pairs={{0,1},{1,2},{2,3},{3,4},{4,5},{5,6},{6,7},{7,8},{8,9},{9,10},{10,1... | collective-permute-start | bytes 589832 | tf_op jit(solution)/shard_map/ppermute | solution.py:226
  3.0 3.6 %collective-permute-start.1 = (f32[3,8,2048]{2,1,0:T(8,128)S(1)}, f32[3,8,2048]{2,1,0:T(8,128)S(1)}, u32[]{:S(2)}, u32[]{:S(2)}) collective-permute-start(f32[3,8,2048]{2,1,0:T(8,128)S(1)} %get-tuple-element.11), channel_id=1, source_target_pairs={{1,0},{2,1},{3,2},{4,3},{5,4},{6,5},{7,6},{8,7},{9,8},{10,9},{11,1... | collective-permute-start | bytes 589832 | tf_op jit(solution)/shard_map/ppermute | solution.py:227
  6.6 0.7 pad_convert_fusion
  7.3 0.7 subtract_convert_fusion
  8.1 0.8 subtract_convert_fusion.1
  8.9 0.0 copy-start.2
  8.9 0.0 copy-start
  8.9 0.0 copy-start.1
  8.9 1.6 %copy.9 = bf16[3,3,256,256]{3,2,1,0:T(8,128)(2,1)S(1)} copy(bf16[3,3,256,256]{2,3,1,0:T(8,128)(2,1)} %bitcast.15) | data formatting | bytes 2359296 | tf_op jit(solution)/shard_map/transpose | solution.py:118
  10.5 0.0 copy-done.2
  10.6 0.1 copy.10
  10.7 0.2 concatenate.10.lw_ref
  11.0 0.0 collective-permute-done.up_ref
  11.0 0.0 collective-permute-done.1.dn_ref
  11.0 0.0 copy-done
  11.0 0.0 copy-done.1
  11.0 4.9 %fine_and_guess.1 = (f32[3,16,2048]{2,1,0:T(8,128)S(1)}, f32[32,8,256]{2,1,0:T(8,128)}) custom-call(s32[1]{0:T(128)} %bitcast.1.tm_ref, f32[1,3,16,2048]{3,2,1,0:T(8,128)S(1)} %copy-done, f32[3,8,2048]{2,1,0:T(8,128)S(1)} %collective-permute-done.up_ref, f32[3,8,2048]{2,1,0:T(8,128)S(1)} %collective-permute-done.1.dn_ref, bf16[3,768,256]{2,1,0:T(8,128)(2,1)S(1)} %bitcast.8, ...), custom_call_target="tpu_custom_call" | custom-call | tf_op jit(solution)/shard_map/fine_and_guess/pallas_call | solution.py:231
  15.9 13.2 %all-to-all-start = ((f32[32,8,256]{2,1,0:T(8,128)}), f32[32,8,256]{2,1,0:T(8,128)S(1)}, u32[]{:S(2)}, u32[]{:S(2)}) async-start(f32[32,8,256]{2,1,0:T(8,128)} %get-tuple-element.7), calls=%async_computation | async-start | bytes 524288 | tf_op jit(solution)/shard_map/all_to_all | solution.py:238
  29.1 12.1 %all-to-all-done.b_ref = f32[32,8,256]{2,1,0:T(8,128)S(1)} async-done(((f32[32,8,256]{2,1,0:T(8,128)}), f32[32,8,256]{2,1,0:T(8,128)S(1)}, u32[]{:S(2)}, u32[]{:S(2)}) %all-to-all-start) | async-done | bytes 262176 | tf_op jit(solution)/shard_map/all_to_all | solution.py:238
  41.2 2.2 %windows.1 = f32[16,4,1536]{2,1,0:T(4,128)S(1)} custom-call(s32[1]{0:T(128)} %bitcast.sp_ref, f32[32,8,256]{2,1,0:T(8,128)S(1)} %all-to-all-done.b_ref), custom_call_target="tpu_custom_call" | custom-call | tf_op jit(solution)/shard_map/windows/pallas_call | solution.py:239
  43.4 24.4 %all_to_all.15.r_ref = f32[16,4,1536]{2,1,0:T(4,128)S(1)} all-to-all(f32[16,4,1536]{2,1,0:T(4,128)S(1)} %windows.1), channel_id=1, replica_groups=mesh['tm'=16,'space'=32] {'tm'}, dimensions={0} | all-to-all | bytes 786432 | tf_op jit(solution)/shard_map/all_to_all | solution.py:243
  67.8 38.2 %shard_map.64 = f32[16,4,32]{2,1,0:T(4,128)S(1)} custom-call(f32[16,4,1536]{2,1,0:T(4,128)S(1)} %all_to_all.15.r_ref, bf16[3,768,256]{2,1,0:T(8,128)(2,1)S(1)} %bitcast.9, bf16[256,256]{1,0:T(8,128)(2,1)S(1)} %concatenate.10.lw_ref, bf16[256,128]{1,0:T(8,128)(2,1)S(1)} %bitcast.12, f32[1,256]{1,0:T(1,128)S(1)} %bitcast.14), custom_call_target="tpu_custom_call" | custom-call | tf_op jit(solution)/shard_map/pallas_call | solution.py:108
  106.1 0.1 reshape.24
  106.2 12.7 %all_to_all.16 = f32[16,1,128]{2,1,0:T(1,128)S(1)} all-to-all(f32[16,1,128]{2,1,0:T(1,128)S(1)} %reshape.24), channel_id=1, replica_groups=mesh['tm'=16,'space'=32] {'tm'}, dimensions={0} | all-to-all | bytes 16384 | tf_op jit(solution)/shard_map/all_to_all | solution.py:245
  118.9 0.5 broadcast.13
  119.4 0.7 reduce
  120.1 0.1 reshape.25.g_ref
  120.1 0.9 correct.1
  (10 shorter events, 0.1 us)
Async XLA Ops:
  1.1 9.9 %collective-permute-start = (f32[3,8,2048]{2,1,0:T(8,128)S(1)}, f32[3,8,2048]{2,1,0:T(8,128)S(1)}, u32[]{:S(2)}, u32[]{:S(2)}) collective-permute-start(f32[3,8,2048]{2,1,0:T(8,128)S(1)} %get-tuple-element.12), channel_id=1, source_target_pairs={{0,1},{1,2},{2,3},{3,4},{4,5},{5,6},{6,7},{7,8},{8,9},{9,10},{10,1... | collective-permute-start | bytes 589832 | tf_op jit(solution)/shard_map/ppermute | solution.py:226
  3.0 8.0 %collective-permute-start.1 = (f32[3,8,2048]{2,1,0:T(8,128)S(1)}, f32[3,8,2048]{2,1,0:T(8,128)S(1)}, u32[]{:S(2)}, u32[]{:S(2)}) collective-permute-start(f32[3,8,2048]{2,1,0:T(8,128)S(1)} %get-tuple-element.11), channel_id=1, source_target_pairs={{1,0},{2,1},{3,2},{4,3},{5,4},{6,5},{7,6},{8,7},{9,8},{10,9},{11,1... | collective-permute-start | bytes 589832 | tf_op jit(solution)/shard_map/ppermute | solution.py:227
  8.9 1.7 %copy-start.2 = (bf16[3,256]{1,0:T(4,128)(2,1)S(1)}, bf16[3,256]{1,0:T(4,128)(2,1)}, u32[]{:S(2)}) copy-start(bf16[3,256]{1,0:T(4,128)(2,1)} %param.11) | copy-start | bytes 4612
  8.9 2.1 %copy-start = (f32[1,3,16,2048]{3,2,1,0:T(8,128)S(1)}, f32[1,3,16,2048]{3,2,1,0:T(8,128)}, u32[]{:S(2)}) copy-start(f32[1,3,16,2048]{3,2,1,0:T(8,128)} %s_ref.1) | copy-start | bytes 1179652
  8.9 2.1 %copy-start.1 = (f32[256]{0:T(256)S(1)}, f32[256]{0:T(256)}, u32[]{:S(2)}) copy-start(f32[256]{0:T(256)} %param.10) | copy-start | bytes 3076
  15.9 25.3 %all-to-all-start = ((f32[32,8,256]{2,1,0:T(8,128)}), f32[32,8,256]{2,1,0:T(8,128)S(1)}, u32[]{:S(2)}, u32[]{:S(2)}) async-start(f32[32,8,256]{2,1,0:T(8,128)} %get-tuple-element.7), calls=%async_computation | async-start | bytes 524288 | tf_op jit(solution)/shard_map/all_to_all | solution.py:238

commit v2 on v1

v2 whole, which is shorter than its diff:
```python
import functools
import jax, jax.numpy as jnp
from jax import lax
from jax.experimental import pallas as pl
from jax.experimental.pallas import tpu as pltpu
from jax.sharding import PartitionSpec as P

f32, bf16 = jnp.float32, jnp.bfloat16
FINE = 4
RF = 8
time_step = 0.2
viscosity = 1.0
sound_sq = 1.0
N = 16
ROWS = 32
W1, W2 = 48, 32

def twice_gelu(x):
    u = x * (0.7978845608028654 + 0.035677408136300125 * (x * x))
    return x + x * jnp.tanh(u)

def lift_operand(s, lane):
    hi = s.astype(bf16)
    lo = (s - hi.astype(f32)).astype(bf16)
    one = jnp.ones_like(hi)
    return jnp.concatenate([jnp.where(lane < 64, hi, lo), jnp.where(lane < 64, hi, one)], axis=1)

def shifted(h, axis_size):
    return pltpu.roll(h, 1, 0), pltpu.roll(h, axis_size - 1, 0)

def chain_kernel(SPLITS, r_ref, wt_ref, lw_ref, ow_ref, cb_ref, out_ref, d_ref, s_ref, top_ref, low_ref, *h_refs):
    part = ROWS * W1 // 4
    acc = r_ref[0]
    d_ref[0:4] = jnp.zeros((4, 3 * part), f32)
    d_ref[4:8] = acc
    for n in range(1, N - 1):
        acc = acc + r_ref[n]
        d_ref[4 * n + 4:4 * n + 8] = acc
    field = lax.broadcasted_iota(jnp.int32, (128, 128), 1) & 3
    for t in range(part // 128):
        turned = [d_ref[:, f * part + t * 128:f * part + t * 128 + 128].T for f in range(3)]
        turned = [jnp.concatenate([x, x], axis=1) for x in turned]
        for u in range(4):
            s = jnp.zeros((128, 128), f32)
            for f in range(3):
                moved = turned[f] if f == u else pltpu.roll(turned[f], (f - u) % 128, 1)
                s = jnp.where(field == f, moved, s)
            s_ref[u * part + t * 128:u * part + t * 128 + 128, :] = s
    krow = lax.broadcasted_iota(jnp.int32, (256, 256), 0)
    kslot = (krow & 63) >> 2
    ocol = (lax.broadcasted_iota(jnp.int32, (256, 128), 1) & 63) >> 2
    lw, ow = lw_ref[...].astype(f32), ow_ref[...].astype(f32)

    def rows_of(row, n, pitch):
        if pitch == W1:
            return [pl.ds(row * W1, n * W1)]
        return [pl.ds((row + i) * W1 + (W1 - pitch) // 2, pitch) for i in range(n)]

    def pitch_of(m):
        return W1 if m < 8 else W2

    def lift(m, lo, hi):
        if hi <= lo:
            return
        n, pitch, h = hi - lo, pitch_of(m), h_refs[m % 2]
        cells = n * pitch
        s = jnp.concatenate([s_ref[d, :] for d in rows_of(lo, n, pitch)], axis=0)
        lane = lax.broadcasted_iota(jnp.int32, s.shape, 1)
        lwm = jnp.where((kslot == m) | (krow >= 192), lw, 0.0).astype(bf16)
        y = twice_gelu(jnp.dot(lift_operand(s, lane), lwm, preferred_element_type=f32))
        left, right = shifted(y, cells)
        dst = pl.ds(lo * pitch, cells)
        h[dst, 0:256] = left.astype(bf16)
        h[dst, 256:512] = y.astype(bf16)
        h[dst, 512:768] = right.astype(bf16)

    def conv(m, lo, hi):
        n, pitch, h = hi - lo, pitch_of(m), h_refs[m % 2]
        x = jnp.concatenate([h[pl.ds((lo + di - 1) * pitch, n * pitch), :] for di in range(3)], axis=1)
        return jnp.dot(x, wt_ref[...].reshape(2304, 256), preferred_element_type=f32)

    def finish(m, lo, hi, acc):
        n, pitch = hi - lo, pitch_of(m)
        act = twice_gelu(acc + cb_ref[...]).astype(bf16)
        owm = jnp.where(ocol >= m, ow, 0.0).astype(bf16)
        inc = jnp.dot(act, owm, preferred_element_type=f32)
        at = 0
        for d in rows_of(lo, n, pitch):
            s_ref[d, :] = s_ref[d, :] + inc[at:at + d.size]
            at += d.size

    splits = SPLITS

    def block(body):
        body()

    def store_conv(m, lo, hi, acc_ref):
        if hi > lo:
            acc_ref[0:(hi - lo) * pitch_of(m), :] = conv(m, lo, hi)

    def finish_from(m, lo, hi, acc_ref):
        if hi > lo:
            finish(m, lo, hi, acc_ref[0:(hi - lo) * pitch_of(m), :])

    lift(1, 0, splits[1] + 1)
    done = splits[1] + 1
    for m in range(1, N + 1):
        prev = (m - 1, splits[m - 1], 33 - m)
        if m == N:
            block(lambda: finish_from(*prev, low_ref))
            break
        lo, hi, b = m, 32 - m, splits[m]
        need = min(b + 1, hi + 1)
        if done < need:
            def catch_up():
                if m > 1:
                    finish_from(*prev, low_ref)
                lift(m, done, need)
            block(catch_up)
            done, prev = need, (m - 1, 0, 0)

        def upper():
            store_conv(m, lo, min(b, hi), top_ref)
            if m > 1:
                finish_from(*prev, low_ref)
            lift(m, done, hi + 1)
        block(upper)
        early = m if m + 1 == N else max(m, min(b, splits[m + 1] + 1))

        def lower():
            store_conv(m, b, hi, low_ref)
            finish_from(m, lo, min(b, hi), top_ref)
            if m + 1 < N:
                lift(m + 1, m, early)
        block(lower)
        done = early
    g = jnp.concatenate([s_ref[15 * W1 + 16:15 * W1 + 32, :], s_ref[16 * W1 + 16:16 * W1 + 32, :]], axis=0)
    gt = g.T
    for n in range(N):
        for f in range(3):
            out_ref[n, :, 32 * f:32 * f + 32] = gt[4 * n + f:4 * n + f + 1, :]
        out_ref[n, :, 96:128] = jnp.zeros((1, 32), f32)

SPLITS = (0, 19, 18, 17, 16, 15, 14, 13, 17, 16, 15, 14, 20, 19, 18, 17)

def chain(recv, wt, lw, ow, cb, SPLITS=SPLITS):
    L = ROWS * W1
    vm = pl.BlockSpec(memory_space=pltpu.VMEM)
    return pl.pallas_call(
        functools.partial(chain_kernel, tuple(SPLITS)),
        out_shape=jax.ShapeDtypeStruct((N, 1, 128), f32),
        in_specs=[vm] * 5, out_specs=vm,
        scratch_shapes=[pltpu.VMEM((64, 3 * L // 4), f32), pltpu.VMEM((L, 128), f32), pltpu.VMEM((L, 256), f32), pltpu.VMEM((L, 256), f32),
                        pltpu.VMEM((L, 768), bf16), pltpu.VMEM((L, 768), bf16)],
        compiler_params=pltpu.CompilerParams(vmem_limit_bytes=48 * 2**20),
    )(recv, wt, lw, ow, cb)

def table_kernel(lwt_ref, lb_ref, cw_ref, ow_ref, wt_ref, lw_ref, owr_ref, wide_ref, rows_ref):
    for i in range(3):
        for j in range(3):
            wt_ref[i, 256 * j:256 * j + 256, :] = (0.5 * cw_ref[i, j].astype(f32)).T.astype(bf16)
    wide_ref[...] = jnp.zeros(wide_ref.shape, f32)
    wide_ref[:, 0:3] = lwt_ref[...]
    w = wide_ref[...].T[0:8]
    hi = w.astype(bf16).astype(f32)
    rows_ref[0:8, :] = hi
    rows_ref[8:16, :] = w - hi
    b = lb_ref[...]
    bhi = b.astype(bf16).astype(f32)
    rows_ref[3:4, :] = bhi
    rows_ref[11:12, :] = b - bhi
    k = lax.broadcasted_iota(jnp.int32, (256, 16), 0)
    col = lax.broadcasted_iota(jnp.int32, (256, 16), 1)
    field = k & 3
    weight = (k < 192) & (field < 3) & (col == field + jnp.where(k < 128, 0, 8))
    bias = ((k == 192) & (col == 3)) | ((k == 193) & (col == 11))
    pick = jnp.where(weight | bias, 1.0, 0.0).astype(bf16)
    lw_ref[...] = jnp.dot(pick, rows_ref[...].astype(bf16), preferred_element_type=f32).astype(bf16)
    rows_ref[...] = jnp.zeros(rows_ref.shape, f32)
    rows_ref[0:3, :] = 0.5 * ow_ref[...].astype(f32)
    lane = lax.broadcasted_iota(jnp.int32, (128, 16), 0) & 3
    pick = jnp.where((lane < 3) & (lane == lax.broadcasted_iota(jnp.int32, (128, 16), 1)), 1.0, 0.0).astype(bf16)
    owr_ref[...] = jnp.dot(pick, rows_ref[...].astype(bf16), preferred_element_type=f32).T.astype(bf16)

def tables(lift_weight, lift_bias, conv_weight, conv_bias, out_weight):
    vm = pl.BlockSpec(memory_space=pltpu.VMEM)
    wt, lw, ow = pl.pallas_call(
        table_kernel,
        out_shape=[jax.ShapeDtypeStruct((3, 768, 256), bf16), jax.ShapeDtypeStruct((256, 256), bf16), jax.ShapeDtypeStruct((256, 128), bf16)],
        in_specs=[vm] * 4, out_specs=[vm] * 3,
        scratch_shapes=[pltpu.VMEM((256, 128), f32), pltpu.VMEM((16, 256), f32)],
        compiler_params=pltpu.CompilerParams(vmem_limit_bytes=32 * 2**20),
        cost_estimate=pl.CostEstimate(flops=10**7, bytes_accessed=10**7, transcendentals=0), name="tables",
    )(lift_weight, lift_bias[None], conv_weight, out_weight)
    return wt, lw, ow, conv_bias[None]

def thirds(x):
    hi = x.astype(bf16)
    rest = x - hi.astype(f32)
    mid = rest.astype(bf16)
    low = (rest - mid.astype(f32)).astype(bf16)
    return jnp.concatenate([hi, mid, low], axis=0)

def exact_dot(x, pattern):
    n = x.shape[0]
    y = jnp.dot(thirds(x), pattern, preferred_element_type=f32)
    return y[0:n] + y[n:2 * n] + y[2 * n:3 * n]

def fine_step(a, b, q):
    def parts(x):
        e, w = pltpu.roll(x, x.shape[1] - 1, 1), pltpu.roll(x, 1, 1)
        n, s = pltpu.roll(x, 1, 0), pltpu.roll(x, x.shape[0] - 1, 0)
        return e - w, s - n, (e + w) + (n + s)
    ax, ay, al = parts(a)
    bx, by, bl = parts(b)
    qx, qy, ql = parts(q)
    half, keep = 0.5 * time_step, 1.0 - 4.0 * time_step * viscosity
    new_a = keep * a + time_step * viscosity * al - half * (a * ax + b * ay + qx)
    new_b = keep * b + time_step * viscosity * bl - half * (a * bx + b * by + qy)
    new_q = keep * q + time_step * viscosity * ql - half * sound_sq * (ax + by)
    return new_a, new_b, new_q

def first_kernel(tm_ref, s_ref, up_ref, dn_ref, wt_ref, lw_ref, ow_ref, cb_ref, corr_ref, c_ref, q_ref, h_ref):
    fields = [jnp.concatenate([up_ref[f], s_ref[0, f], dn_ref[f]], axis=0) for f in range(3)]
    q_ref[...] = jnp.zeros(q_ref.shape, f32)
    for f in range(3):
        for r in range(4):
            q_ref[4 * r + f:4 * r + f + 1, :] = jnp.sum(fields[f][8 * r:8 * r + 8], axis=0, keepdims=True)
    for _ in range(FINE):
        fields = fine_step(*fields)
    for f in range(3):
        for r in range(2):
            q_ref[16 + 4 * r + f:17 + 4 * r + f, :] = jnp.sum(fields[f][8 + 8 * r:16 + 8 * r], axis=0, keepdims=True)
    half = 128 * RF
    pool = (lax.broadcasted_iota(jnp.int32, (half, 128), 0) // RF == lax.broadcasted_iota(jnp.int32, (half, 128), 1)).astype(f32).astype(bf16)
    spread = (lax.broadcasted_iota(jnp.int32, (128, half), 1) // RF == lax.broadcasted_iota(jnp.int32, (128, half), 0)).astype(f32).astype(bf16)
    pooled = jnp.concatenate([exact_dot(q_ref[:, 0:half], pool), exact_dot(q_ref[:, half:], pool)], axis=1) * (1.0 / (RF * RF))
    pad = jnp.zeros((48, 256), f32)
    s = jnp.concatenate([pooled[0:16], pad, pooled[0:16], pad], axis=0).T
    x = lift_operand(s, lax.broadcasted_iota(jnp.int32, s.shape, 1))
    krow = lax.broadcasted_iota(jnp.int32, (256, 256), 0)
    kslot = (krow & 63) >> 2
    lw = lw_ref[...].astype(f32)
    for r in range(4):
        lwm = jnp.where((kslot == r) | (krow >= 192), lw, 0.0).astype(bf16)
        h = twice_gelu(jnp.dot(x, lwm, preferred_element_type=f32))
        left, right = shifted(h, 256)
        h_ref[256 * r:256 * r + 256, 0:256] = left.astype(bf16)
        h_ref[256 * r:256 * r + 256, 256:512] = h.astype(bf16)
        h_ref[256 * r:256 * r + 256, 512:768] = right.astype(bf16)
    acc = jnp.dot(h_ref[0:512], wt_ref[0], preferred_element_type=f32)
    acc = acc + jnp.dot(h_ref[256:768], wt_ref[1], preferred_element_type=f32)
    acc = acc + jnp.dot(h_ref[512:1024], wt_ref[2], preferred_element_type=f32)
    act = twice_gelu(acc + cb_ref[...]).astype(bf16)
    inc = jnp.dot(act, ow_ref[...], preferred_element_type=f32)
    lane = lax.broadcasted_iota(jnp.int32, s.shape, 1)
    guess = (s + jnp.where(lane < 8, inc[0:256], inc[256:512])).T[4:12]
    first = jnp.where(tm_ref[0] == 0, guess, 0.0)
    c = first + (pooled[16:24] - guess)
    for i in range(c_ref.shape[0]):
        c_ref[i] = c
    delta = guess - first
    for p in range(2):
        wide = exact_dot(delta[:, 128 * p:128 * p + 128], spread)
        for f in range(3):
            for r in range(2):
                corr_ref[f, 8 * r:8 * r + 8, half * p:half * p + half] = fields[f][8 + 8 * r:16 + 8 * r, half * p:half * p + half] - wide[4 * r + f:4 * r + f + 1]

def window_kernel(sp_ref, b_ref, out_ref, w_ref):
    count = b_ref.shape[0]
    for q in range(ROWS):
        dev = lax.rem(sp_ref[0] + (count - 8 + (q + 1) // 2), count)
        r = (q + 1) % 2
        for f in range(3):
            w_ref[3 * (q % 8) + f, q // 8:q // 8 + 1, :] = b_ref[dev, 4 * r + f:4 * r + f + 1, :]
    for i in range(8):
        for f in range(3):
            v = w_ref[3 * i + f]
            ext = jnp.concatenate([v[:, 240:256], v, v[:, 0:16]], axis=1)
            at = f * 8 * W1 + i * W1
            for j in range(N):
                out_ref[j, :, at:at + W1] = ext[:, 16 * j:16 * j + W1]

def last_kernel(g_ref, corr_ref, out_ref, y_ref):
    for j in range(N):
        y_ref[j:j + 1, :] = g_ref[j]
    parts = thirds(y_ref[...])
    row = lax.broadcasted_iota(jnp.int32, (128, 128), 0)
    col = lax.broadcasted_iota(jnp.int32, (128, 128), 1)
    for r in range(2):
        for f in range(3):
            pattern = (row - 32 * f - 16 * r == col // RF).astype(f32).astype(bf16)
            y = jnp.dot(parts, pattern, preferred_element_type=f32)
            y = y[0:N] + y[N:2 * N] + y[2 * N:3 * N]
            for j in range(N):
                at = 128 * j
                out_ref[0, f, 8 * r:8 * r + 8, at:at + 128] = corr_ref[f, 8 * r:8 * r + 8, at:at + 128] + y[j:j + 1]

def shards(start_states, lift_weight, lift_bias, conv_weight, conv_bias, out_weight):
    vm = pl.BlockSpec(memory_space=pltpu.VMEM)
    sm = pl.BlockSpec(memory_space=pltpu.SMEM)
    params = pltpu.CompilerParams(vmem_limit_bytes=48 * 2**20)
    count = lax.axis_size("space")
    slab = start_states[0]
    up = lax.ppermute(slab[:, 8:], "space", [(i, (i + 1) % count) for i in range(count)])
    down = lax.ppermute(slab[:, :8], "space", [((i + 1) % count, i) for i in range(count)])
    weights = tables(lift_weight, lift_bias, conv_weight, conv_bias, out_weight)
    tm = lax.axis_index("tm").astype(jnp.int32).reshape(1)
    sp = lax.axis_index("space").astype(jnp.int32).reshape(1)
    corr, c = pl.pallas_call(
        first_kernel,
        out_shape=[jax.ShapeDtypeStruct(slab.shape, f32), jax.ShapeDtypeStruct((count, 8, 256), f32)],
        in_specs=[sm] + [vm] * 7, out_specs=[vm, vm],
        scratch_shapes=[pltpu.VMEM((24, slab.shape[2]), f32), pltpu.VMEM((1024, 768), bf16)],
        compiler_params=params, name="fine_and_guess",
    )(tm, start_states, up, down, *weights)
    c = lax.all_to_all(c, "space", 0, 0)
    send = pl.pallas_call(
        window_kernel, out_shape=jax.ShapeDtypeStruct((N, 4, 3 * ROWS * W1 // 4), f32),
        in_specs=[sm, vm], out_specs=vm, scratch_shapes=[pltpu.VMEM((24, 4, 256), f32)],
        compiler_params=params, name="windows",
    )(sp, c)
    recv = lax.all_to_all(send, "tm", 0, 0)
    g = chain(recv, *weights)
    g = lax.all_to_all(g, "tm", 0, 0)
    return pl.pallas_call(
        last_kernel, out_shape=jax.ShapeDtypeStruct(start_states.shape, f32),
        in_specs=[vm, vm], out_specs=vm, scratch_shapes=[pltpu.VMEM((N, 128), f32)],
        compiler_params=params, name="correct",
    )(g, corr)

def solution(mesh):
    return jax.shard_map(
        shards, mesh=mesh,
        in_specs=(P("tm", None, "space", None), P(), P(), P(), P(), P()),
        out_specs=P("tm", None, "space", None), check_vma=False,
    )
```

time: 122 us -> 104 us (0.85)
  Pallas kernels: 46.3 us -> 32 us
  waiting for transfers between devices: 12.1 us -> 16.9 us
  starting transfers between devices: 18.8 us -> 15.6 us
  blocking collectives: 37.1 us -> 34.8 us
  other arithmetic: 2.12 us -> 0 us
    pallas_call x2 -> x3, Pallas kernels: 40.5 us -> 26.2 us  [the longest x1 24.1 us: chain(): pl.pallas_call(functools.partial(chain_kernel, tuple(SPLITS)), out_shape=...]
    ppermute x1, waiting for transfers between devices: 0.01 us -> 4.78 us  [shards(): lax.ppermute(slab[:, 8:], 'space', [(i, (i + 1) % count) for i in range(c...]
    unnamed x8 -> x11, local copies, waits for them, and re-layouts: 0.19 us -> 3.45 us
    all_to_all x1, blocking collectives: 24.4 us -> 22.3 us  [shards(): recv = lax.all_to_all(send, 'tm', 0, 0)]
    all_to_all x1, starting transfers between devices: 13.2 us -> 11.3 us  [shards(): c = lax.all_to_all(c, 'space', 0, 0)]
    ppermute x1, starting transfers between devices: 3.64 us -> 1.92 us  [shards(): lax.ppermute(slab[:, :8], 'space', [((i + 1) % count, i) for i in range(c...]
    transpose x1 -> x0, local copies, waits for them, and re-layouts: 1.62 us -> none  [tables(): wt = conv_weight.transpose(0, 1, 3, 2).reshape(3, 768, 256)]
    convert_element_type x2 -> x0, other arithmetic: 1.45 us -> none  [the longest x1 0.76 us: tables(): bl = (lift_bias - bh.astype(f32)).astype(bf16)]
  transfers between devices with their start and end apart: 3 -> 3, of which waited for: 1 -> 2; matrix products, arithmetic and copies ran while one was open for 4% -> 1% of each run, Pallas kernels for 0% -> 1%
where the time goes in v2:
time: 104 us
  blocking collectives  34.8 us (33%)
  Pallas kernels  32 us (31%)
  waiting for transfers between devices  16.9 us (16%)
  starting transfers between devices  15.6 us (15%)
  local copies, waits for them, and re-layouts  4.55 us (4%)
    pallas_call x1, Pallas kernels, chain(): pl.pallas_call(functools.partial(chain_kernel, tuple(SPLITS)), out_shape=...  24.1 us
    all_to_all x1, blocking collectives, shards(): recv = lax.all_to_all(send, 'tm', 0, 0)  22.3 us
    all_to_all x1, blocking collectives, shards(): g = lax.all_to_all(g, 'tm', 0, 0)  12.5 us
    all_to_all x1, waiting for transfers between devices, shards(): c = lax.all_to_all(c, 'space', 0, 0)  12.2 us
    all_to_all x1, starting transfers between devices, shards(): c = lax.all_to_all(c, 'space', 0, 0)  11.3 us
    ppermute x1, waiting for transfers between devices, shards(): lax.ppermute(slab[:, 8:], 'space', [(i, (i + 1) % count) for i in range(c...  4.78 us
    pallas_call x1, Pallas kernels, shards(): pl.pallas_call(first_kernel, out_shape=[jax.ShapeDtypeStruct(slab.shape,...  4.76 us
    unnamed x11, local copies, waits for them, and re-layouts  3.45 us
  transfers between devices with their start and end apart: 3, of which 2 were waited for; matrix products, arithmetic and copies ran while one was open for 1% of the time, Pallas kernels for 1%

profile of v2, /device:TPU:2, one launch (start us, length us, event | category | flops | bytes accessed | tf_op | source)
XLA Modules:
  0.0 104.0 jit_solution(12201255261335890834)
XLA Ops:
  0.0 0.0 copy-start
  0.0 0.0 copy-start.2
  0.0 1.1 %fusion = (f32[3,8,2048]{2,1,0:T(8,128)S(1)}, f32[3,8,2048]{2,1,0:T(8,128)S(1)}) fusion(f32[3,16,2048]{2,1,0:T(8,128)} %bitcast.5), kind=kLoop, calls=%fused_computation | loop fusion | bytes 786432 | tf_op jit(solution)/shard_map/slice | solution.py:306
  1.1 1.9 %collective-permute-start.1 = (f32[3,8,2048]{2,1,0:T(8,128)S(1)}, f32[3,8,2048]{2,1,0:T(8,128)S(1)}, u32[]{:S(2)}, u32[]{:S(2)}) collective-permute-start(f32[3,8,2048]{2,1,0:T(8,128)S(1)} %get-tuple-element.15), channel_id=1, source_target_pairs={{1,0},{2,1},{3,2},{4,3},{5,4},{6,5},{7,6},{8,7},{9,8},{10,9},{11,1... | collective-permute-start | bytes 589832 | tf_op jit(solution)/shard_map/ppermute | solution.py:306
  3.0 2.4 %collective-permute-start = (f32[3,8,2048]{2,1,0:T(8,128)S(1)}, f32[3,8,2048]{2,1,0:T(8,128)S(1)}, u32[]{:S(2)}, u32[]{:S(2)}) collective-permute-start(f32[3,8,2048]{2,1,0:T(8,128)S(1)} %get-tuple-element.16), channel_id=1, source_target_pairs={{0,1},{1,2},{2,3},{3,4},{4,5},{5,6},{6,7},{7,8},{8,9},{9,10},{10,1... | collective-permute-start | bytes 589832 | tf_op jit(solution)/shard_map/ppermute | solution.py:305
  5.5 0.8 copy.7.lwt_ref
  6.3 0.0 copy-start.1
  6.3 1.3 %copy-done.1 = bf16[3,3,256,256]{3,2,1,0:T(8,128)(2,1)S(1)} copy-done((bf16[3,3,256,256]{3,2,1,0:T(8,128)(2,1)S(1)}, bf16[3,3,256,256]{3,2,1,0:T(8,128)(2,1)}, u32[]{:S(2)}) %copy-start.1) | copy-done | bytes 1179672
  7.6 0.0 copy-start.3
  7.6 0.7 copy-done.3
  8.2 0.0 copy-start.4
  8.2 0.7 copy-done.4
  8.9 0.6 tables.1
  9.5 0.0 collective-permute-done.1.dn_ref
  9.5 4.8 %collective-permute-done.up_ref = f32[3,8,2048]{2,1,0:T(8,128)S(1)} collective-permute-done((f32[3,8,2048]{2,1,0:T(8,128)S(1)}, f32[3,8,2048]{2,1,0:T(8,128)S(1)}, u32[]{:S(2)}, u32[]{:S(2)}) %collective-permute-start) | collective-permute-done | bytes 196640 | tf_op jit(solution)/shard_map/ppermute | solution.py:305
  14.3 0.0 copy-done
  14.3 0.0 copy-done.2
  14.3 4.8 %fine_and_guess.1 = (f32[3,16,2048]{2,1,0:T(8,128)S(1)}, f32[32,8,256]{2,1,0:T(8,128)}) custom-call(s32[1]{0:T(128)} %bitcast.1.tm_ref, f32[1,3,16,2048]{3,2,1,0:T(8,128)S(1)} %copy-done, f32[3,8,2048]{2,1,0:T(8,128)S(1)} %collective-permute-done.up_ref, f32[3,8,2048]{2,1,0:T(8,128)S(1)} %collective-permute-done.1.dn_ref, ...), custom_call_target="tpu_custom_call" | custom-call | tf_op jit(solution)/shard_map/fine_and_guess/pallas_call | solution.py:310
  19.1 11.3 %all-to-all-start = ((f32[32,8,256]{2,1,0:T(8,128)}), f32[32,8,256]{2,1,0:T(8,128)S(1)}, u32[]{:S(2)}, u32[]{:S(2)}) async-start(f32[32,8,256]{2,1,0:T(8,128)} %get-tuple-element.13), calls=%async_computation | async-start | bytes 524288 | tf_op jit(solution)/shard_map/all_to_all | solution.py:317
  30.4 12.2 %all-to-all-done.b_ref = f32[32,8,256]{2,1,0:T(8,128)S(1)} async-done(((f32[32,8,256]{2,1,0:T(8,128)}), f32[32,8,256]{2,1,0:T(8,128)S(1)}, u32[]{:S(2)}, u32[]{:S(2)}) %all-to-all-start) | async-done | bytes 262176 | tf_op jit(solution)/shard_map/all_to_all | solution.py:317
  42.5 1.6 %windows.1 = f32[16,4,1152]{2,1,0:T(4,128)S(1)} custom-call(s32[1]{0:T(128)} %bitcast.sp_ref, f32[32,8,256]{2,1,0:T(8,128)S(1)} %all-to-all-done.b_ref), custom_call_target="tpu_custom_call" | custom-call | tf_op jit(solution)/shard_map/windows/pallas_call | solution.py:318
  44.1 22.3 %all_to_all.15.r_ref = f32[16,4,1152]{2,1,0:T(4,128)S(1)} all-to-all(f32[16,4,1152]{2,1,0:T(4,128)S(1)} %windows.1), channel_id=1, replica_groups=mesh['tm'=16,'space'=32] {'tm'}, dimensions={0} | all-to-all | bytes 589824 | tf_op jit(solution)/shard_map/all_to_all | solution.py:323
  66.4 24.1 %shard_map.64 = f32[16,1,128]{2,1,0:T(1,128)S(1)} custom-call(f32[16,4,1152]{2,1,0:T(4,128)S(1)} %all_to_all.15.r_ref, bf16[3,768,256]{2,1,0:T(8,128)(2,1)S(1)} %get-tuple-element.10.wt_ref, bf16[256,256]{1,0:T(8,128)(2,1)S(1)} %get-tuple-element.11.lw_ref, bf16[256,128]{1,0:T(8,128)(2,1)S(1)} %get-tuple-element.12.ow_ref, f32[1,256]{1,0:T(1,128)S(1)} %bitcast.7), custom_call_target="tpu_custom_call" | custom-call | tf_op jit(solution)/shard_map/pallas_call | solution.py:149
  90.5 12.5 %all_to_all.16.g_ref = f32[16,1,128]{2,1,0:T(1,128)S(1)} all-to-all(f32[16,1,128]{2,1,0:T(1,128)S(1)} %shard_map.64), channel_id=1, replica_groups=mesh['tm'=16,'space'=32] {'tm'}, dimensions={0} | all-to-all | bytes 16384 | tf_op jit(solution)/shard_map/all_to_all | solution.py:325
  103.0 1.0 correct.1
Async XLA Ops:
  0.0 14.3 %copy-start = (f32[1,3,16,2048]{3,2,1,0:T(8,128)S(1)}, f32[1,3,16,2048]{3,2,1,0:T(8,128)}, u32[]{:S(2)}) copy-start(f32[1,3,16,2048]{3,2,1,0:T(8,128)} %s_ref.1) | copy-start | bytes 1179652
  0.0 14.3 %copy-start.2 = (f32[256]{0:T(256)S(1)}, f32[256]{0:T(256)}, u32[]{:S(2)}) copy-start(f32[256]{0:T(256)} %param.10) | copy-start | bytes 3076
  1.1 8.4 %collective-permute-start.1 = (f32[3,8,2048]{2,1,0:T(8,128)S(1)}, f32[3,8,2048]{2,1,0:T(8,128)S(1)}, u32[]{:S(2)}, u32[]{:S(2)}) collective-permute-start(f32[3,8,2048]{2,1,0:T(8,128)S(1)} %get-tuple-element.15), channel_id=1, source_target_pairs={{1,0},{2,1},{3,2},{4,3},{5,4},{6,5},{7,6},{8,7},{9,8},{10,9},{11,1... | collective-permute-start | bytes 589832 | tf_op jit(solution)/shard_map/ppermute | solution.py:306
  3.0 11.3 %collective-permute-start = (f32[3,8,2048]{2,1,0:T(8,128)S(1)}, f32[3,8,2048]{2,1,0:T(8,128)S(1)}, u32[]{:S(2)}, u32[]{:S(2)}) collective-permute-start(f32[3,8,2048]{2,1,0:T(8,128)S(1)} %get-tuple-element.16), channel_id=1, source_target_pairs={{0,1},{1,2},{2,3},{3,4},{4,5},{5,6},{6,7},{7,8},{8,9},{9,10},{10,1... | collective-permute-start | bytes 589832 | tf_op jit(solution)/shard_map/ppermute | solution.py:305
  6.3 1.3 %copy-start.1 = (bf16[3,3,256,256]{3,2,1,0:T(8,128)(2,1)S(1)}, bf16[3,3,256,256]{3,2,1,0:T(8,128)(2,1)}, u32[]{:S(2)}) copy-start(bf16[3,3,256,256]{3,2,1,0:T(8,128)(2,1)} %cw_ref.1) | copy-start | bytes 3538948
  7.6 0.7 copy-start.3
  8.2 0.7 copy-start.4
  19.1 23.5 %all-to-all-start = ((f32[32,8,256]{2,1,0:T(8,128)}), f32[32,8,256]{2,1,0:T(8,128)S(1)}, u32[]{:S(2)}, u32[]{:S(2)}) async-start(f32[32,8,256]{2,1,0:T(8,128)} %get-tuple-element.13), calls=%async_computation | async-start | bytes 524288 | tf_op jit(solution)/shard_map/all_to_all | solution.py:317

commit v3 on v2

--- a/solution.py
+++ b/solution.py
@@ -28,7 +28,7 @@
 def shifted(h, axis_size):
     return pltpu.roll(h, 1, 0), pltpu.roll(h, axis_size - 1, 0)
 
-def chain_kernel(SPLITS, r_ref, wt_ref, lw_ref, ow_ref, cb_ref, out_ref, d_ref, s_ref, top_ref, low_ref, *h_refs):
+def chain_kernel(SPLITS, PIECE, ROLL, r_ref, wt_ref, lw_ref, ow_ref, cb_ref, out_ref, d_ref, s_ref, top_ref, low_ref, y_ref, *h_refs):
     part = ROWS * W1 // 4
     acc = r_ref[0]
     d_ref[0:4] = jnp.zeros((4, 3 * part), f32)
@@ -68,7 +68,8 @@
         lane = lax.broadcasted_iota(jnp.int32, s.shape, 1)
         lwm = jnp.where((kslot == m) | (krow >= 192), lw, 0.0).astype(bf16)
         y = twice_gelu(jnp.dot(lift_operand(s, lane), lwm, preferred_element_type=f32))
-        left, right = shifted(y, cells)
+        y_ref[8:8 + cells, :] = y
+        left, right = y_ref[7:7 + cells, :], y_ref[9:9 + cells, :]
         dst = pl.ds(lo * pitch, cells)
         h[dst, 0:256] = left.astype(bf16)
         h[dst, 256:512] = y.astype(bf16)
@@ -89,6 +90,38 @@
             s_ref[d, :] = s_ref[d, :] + inc[at:at + d.size]
             at += d.size
 
+    def finish_lift(m, lo, hi, acc_ref):
+        pitch, h = pitch_of(m), h_refs[(m + 1) % 2]
+        lwm = jnp.where((kslot == m + 1) | (krow >= 192), lw, 0.0).astype(bf16)
+        owm = jnp.where(ocol >= m, ow, 0.0).astype(bf16)
+        count = max(1, round((hi - lo) * pitch / PIECE))
+        cuts = [lo + (hi - lo) * i // count for i in range(count + 1)]
+        for p, (at, end) in enumerate(zip(cuts[:-1], cuts[1:])):
+            if end <= at:
+                continue
+            cells, base = (end - at) * pitch, (at - lo) * pitch
+            act = twice_gelu(acc_ref[base:base + cells, :] + cb_ref[...]).astype(bf16)
+            inc = jnp.dot(act, owm, preferred_element_type=f32)
+            news, off = [], 0
+            for d in rows_of(at, end - at, pitch):
+                new = s_ref[d, :] + inc[off:off + d.size]
+                s_ref[d, :] = new
+                news.append(new)
+                off += d.size
+            s = jnp.concatenate(news, axis=0)
+            lane = lax.broadcasted_iota(jnp.int32, s.shape, 1)
+            y = twice_gelu(jnp.dot(lift_operand(s, lane), lwm, preferred_element_type=f32))
+            dst = pl.ds(at * pitch, cells)
+            if ROLL:
+                left, right = shifted(y, cells)
+            else:
+                top = 8 + at * pitch + 16 * p
+                y_ref[top:top + cells, :] = y
+                left, right = y_ref[top - 1:top - 1 + cells, :], y_ref[top + 1:top + 1 + cells, :]
+            h[dst, 0:256] = left.astype(bf16)
+            h[dst, 256:512] = y.astype(bf16)
+            h[dst, 512:768] = right.astype(bf16)
+
     splits = SPLITS
 
     def block(body):
@@ -102,38 +135,39 @@
         if hi > lo:
             finish(m, lo, hi, acc_ref[0:(hi - lo) * pitch_of(m), :])
 
+    def fits(m, lo, hi, row, end):
+        return m + 1 < N and pitch_of(m + 1) == pitch_of(m) and row == lo and end == hi
+
     lift(1, 0, splits[1] + 1)
     done = splits[1] + 1
-    for m in range(1, N + 1):
-        prev = (m - 1, splits[m - 1], 33 - m)
-        if m == N:
-            block(lambda: finish_from(*prev, low_ref))
-            break
-        lo, hi, b = m, 32 - m, splits[m]
-        need = min(b + 1, hi + 1)
+    pending = None
+    for m in range(1, N):
+        lo, hi, b = m, 32 - m, min(splits[m], 32 - m)
+        need = b + 1
         if done < need:
-            def catch_up():
-                if m > 1:
-                    finish_from(*prev, low_ref)
-                lift(m, done, need)
-            block(catch_up)
-            done, prev = need, (m - 1, 0, 0)
-
-        def upper():
-            store_conv(m, lo, min(b, hi), top_ref)
-            if m > 1:
-                finish_from(*prev, low_ref)
+            if pending:
+                finish_from(*pending, low_ref)
+                pending = None
+            lift(m, done, need)
+            done = need
+        store_conv(m, lo, b, top_ref)
+        if pending and fits(*pending, done, hi + 1):
+            finish_lift(*pending, low_ref)
+        else:
+            if pending:
+                finish_from(*pending, low_ref)
             lift(m, done, hi + 1)
-        block(upper)
+        pending = (m, b, hi)
         early = m if m + 1 == N else max(m, min(b, splits[m + 1] + 1))
-
-        def lower():
-            store_conv(m, b, hi, low_ref)
-            finish_from(m, lo, min(b, hi), top_ref)
+        store_conv(m, b, hi, low_ref)
+        if b > lo and fits(m, lo, b, m, early):
+            finish_lift(m, lo, b, top_ref)
+        else:
+            finish_from(m, lo, b, top_ref)
             if m + 1 < N:
                 lift(m + 1, m, early)
-        block(lower)
         done = early
+    finish_from(*pending, low_ref)
     g = jnp.concatenate([s_ref[15 * W1 + 16:15 * W1 + 32, :], s_ref[16 * W1 + 16:16 * W1 + 32, :]], axis=0)
     gt = g.T
     for n in range(N):
@@ -143,14 +177,14 @@
 
 SPLITS = (0, 19, 18, 17, 16, 15, 14, 13, 17, 16, 15, 14, 20, 19, 18, 17)
 
-def chain(recv, wt, lw, ow, cb, SPLITS=SPLITS):
+def chain(recv, wt, lw, ow, cb, SPLITS=SPLITS, PIECE=384, ROLL=False):
     L = ROWS * W1
     vm = pl.BlockSpec(memory_space=pltpu.VMEM)
     return pl.pallas_call(
-        functools.partial(chain_kernel, tuple(SPLITS)),
+        functools.partial(chain_kernel, tuple(SPLITS), PIECE, ROLL),
         out_shape=jax.ShapeDtypeStruct((N, 1, 128), f32),
         in_specs=[vm] * 5, out_specs=vm,
-        scratch_shapes=[pltpu.VMEM((64, 3 * L // 4), f32), pltpu.VMEM((L, 128), f32), pltpu.VMEM((L, 256), f32), pltpu.VMEM((L, 256), f32),
+        scratch_shapes=[pltpu.VMEM((64, 3 * L // 4), f32), pltpu.VMEM((L, 128), f32), pltpu.VMEM((L, 256), f32), pltpu.VMEM((L, 256), f32), pltpu.VMEM((L + 16 * 16, 256), f32),
                         pltpu.VMEM((L, 768), bf16), pltpu.VMEM((L, 768), bf16)],
         compiler_params=pltpu.CompilerParams(vmem_limit_bytes=48 * 2**20),
     )(recv, wt, lw, ow, cb)
@@ -220,27 +254,39 @@
     new_q = keep * q + time_step * viscosity * ql - half * sound_sq * (ax + by)
     return new_a, new_b, new_q
 
-def first_kernel(tm_ref, s_ref, up_ref, dn_ref, wt_ref, lw_ref, ow_ref, cb_ref, corr_ref, c_ref, q_ref, h_ref):
-    fields = [jnp.concatenate([up_ref[f], s_ref[0, f], dn_ref[f]], axis=0) for f in range(3)]
+def edge_kernel(s_ref, up_ref, down_ref):
+    up_ref[3, 3:4, :] = jnp.zeros((1, s_ref.shape[3]), f32)
+    down_ref[3, 3:4, :] = jnp.zeros((1, s_ref.shape[3]), f32)
+    for f in range(3):
+        up_ref[f] = s_ref[0, f, 12:16, :]
+        up_ref[3, f:f + 1, :] = jnp.sum(s_ref[0, f, 8:16, :], axis=0, keepdims=True)
+        down_ref[f] = s_ref[0, f, 0:4, :]
+        down_ref[3, f:f + 1, :] = jnp.sum(s_ref[0, f, 0:8, :], axis=0, keepdims=True)
+
+def first_kernel(tm_ref, s_ref, up_ref, dn_ref, wt_ref, lw_ref, ow_ref, cb_ref, corr_ref, c_ref, q_ref, qf_ref, h_ref):
+    blank = jnp.zeros((4, s_ref.shape[3]), f32)
+    fields = [jnp.concatenate([blank, up_ref[f], s_ref[0, f], dn_ref[f], blank], axis=0) for f in range(3)]
     q_ref[...] = jnp.zeros(q_ref.shape, f32)
-    for f in range(3):
-        for r in range(4):
-            q_ref[4 * r + f:4 * r + f + 1, :] = jnp.sum(fields[f][8 * r:8 * r + 8], axis=0, keepdims=True)
-    for _ in range(FINE):
-        fields = fine_step(*fields)
+    qf_ref[...] = jnp.zeros(qf_ref.shape, f32)
+    q_ref[0:4, :] = up_ref[3]
+    q_ref[12:16, :] = dn_ref[3]
     for f in range(3):
         for r in range(2):
-            q_ref[16 + 4 * r + f:17 + 4 * r + f, :] = jnp.sum(fields[f][8 + 8 * r:16 + 8 * r], axis=0, keepdims=True)
+            q_ref[4 + 4 * r + f:5 + 4 * r + f, :] = jnp.sum(s_ref[0, f, 8 * r:8 * r + 8, :], axis=0, keepdims=True)
     half = 128 * RF
     pool = (lax.broadcasted_iota(jnp.int32, (half, 128), 0) // RF == lax.broadcasted_iota(jnp.int32, (half, 128), 1)).astype(f32).astype(bf16)
     spread = (lax.broadcasted_iota(jnp.int32, (128, half), 1) // RF == lax.broadcasted_iota(jnp.int32, (128, half), 0)).astype(f32).astype(bf16)
-    pooled = jnp.concatenate([exact_dot(q_ref[:, 0:half], pool), exact_dot(q_ref[:, half:], pool)], axis=1) * (1.0 / (RF * RF))
+
+    def pooled(ref):
+        return jnp.concatenate([exact_dot(ref[:, 0:half], pool), exact_dot(ref[:, half:], pool)], axis=1) * (1.0 / (RF * RF))
+    start = pooled(q_ref)
     pad = jnp.zeros((48, 256), f32)
-    s = jnp.concatenate([pooled[0:16], pad, pooled[0:16], pad], axis=0).T
+    s = jnp.concatenate([start, pad, start, pad], axis=0).T
     x = lift_operand(s, lax.broadcasted_iota(jnp.int32, s.shape, 1))
     krow = lax.broadcasted_iota(jnp.int32, (256, 256), 0)
     kslot = (krow & 63) >> 2
     lw = lw_ref[...].astype(f32)
+    fields = fine_step(*fields)
     for r in range(4):
         lwm = jnp.where((kslot == r) | (krow >= 192), lw, 0.0).astype(bf16)
         h = twice_gelu(jnp.dot(x, lwm, preferred_element_type=f32))
@@ -248,15 +294,22 @@
         h_ref[256 * r:256 * r + 256, 0:256] = left.astype(bf16)
         h_ref[256 * r:256 * r + 256, 256:512] = h.astype(bf16)
         h_ref[256 * r:256 * r + 256, 512:768] = right.astype(bf16)
+    fields = fine_step(*fields)
     acc = jnp.dot(h_ref[0:512], wt_ref[0], preferred_element_type=f32)
     acc = acc + jnp.dot(h_ref[256:768], wt_ref[1], preferred_element_type=f32)
     acc = acc + jnp.dot(h_ref[512:1024], wt_ref[2], preferred_element_type=f32)
+    fields = fine_step(*fields)
     act = twice_gelu(acc + cb_ref[...]).astype(bf16)
     inc = jnp.dot(act, ow_ref[...], preferred_element_type=f32)
     lane = lax.broadcasted_iota(jnp.int32, s.shape, 1)
     guess = (s + jnp.where(lane < 8, inc[0:256], inc[256:512])).T[4:12]
+    for _ in range(FINE - 3):
+        fields = fine_step(*fields)
+    for f in range(3):
+        for r in range(2):
+            qf_ref[4 * r + f:4 * r + f + 1, :] = jnp.sum(fields[f][8 + 8 * r:16 + 8 * r], axis=0, keepdims=True)
     first = jnp.where(tm_ref[0] == 0, guess, 0.0)
-    c = first + (pooled[16:24] - guess)
+    c = first + (pooled(qf_ref) - guess)
     for i in range(c_ref.shape[0]):
         c_ref[i] = c
     delta = guess - first
@@ -302,8 +355,10 @@
     params = pltpu.CompilerParams(vmem_limit_bytes=48 * 2**20)
     count = lax.axis_size("space")
     slab = start_states[0]
-    up = lax.ppermute(slab[:, 8:], "space", [(i, (i + 1) % count) for i in range(count)])
-    down = lax.ppermute(slab[:, :8], "space", [((i + 1) % count, i) for i in range(count)])
+    edges = jax.ShapeDtypeStruct((4, 4, slab.shape[2]), f32)
+    up, down = pl.pallas_call(edge_kernel, out_shape=[edges, edges], in_specs=[vm], out_specs=[vm, vm], compiler_params=params, name="edges")(start_states)
+    up = lax.ppermute(up, "space", [(i, (i + 1) % count) for i in range(count)])
+    down = lax.ppermute(down, "space", [((i + 1) % count, i) for i in range(count)])
     weights = tables(lift_weight, lift_bias, conv_weight, conv_bias, out_weight)
     tm = lax.axis_index("tm").astype(jnp.int32).reshape(1)
     sp = lax.axis_index("space").astype(jnp.int32).reshape(1)
@@ -311,7 +366,7 @@
         first_kernel,
         out_shape=[jax.ShapeDtypeStruct(slab.shape, f32), jax.ShapeDtypeStruct((count, 8, 256), f32)],
         in_specs=[sm] + [vm] * 7, out_specs=[vm, vm],
-        scratch_shapes=[pltpu.VMEM((24, slab.shape[2]), f32), pltpu.VMEM((1024, 768), bf16)],
+        scratch_shapes=[pltpu.VMEM((16, slab.shape[2]), f32), pltpu.VMEM((8, slab.shape[2]), f32), pltpu.VMEM((1024, 768), bf16)],
         compiler_params=params, name="fine_and_guess",
     )(tm, start_states, up, down, *weights)
     c = lax.all_to_all(c, "space", 0, 0)

time: 104 us -> 102 us (0.981)
  waiting for transfers between devices: 16.9 us -> 12.1 us
  starting transfers between devices: 15.6 us -> 18.8 us
    ppermute x2, waiting for transfers between devices: 4.79 us -> 0.01 us  [the longest x1 0.01 us: shards(): lax.ppermute(down, 'space', [((i + 1) % count, i) for i in range(count)])]
    all_to_all x1, starting transfers between devices: 11.3 us -> 13.1 us  [shards(): c = lax.all_to_all(c, 'space', 0, 0)]
    ppermute x2, starting transfers between devices: 4.33 us -> 5.69 us  [the longest x1 3.64 us: shards(): lax.ppermute(down, 'space', [((i + 1) % count, i) for i in range(count)])]
    slice x1 -> x0, local copies, waits for them, and re-layouts: 1.1 us -> none  [shards(): slab[:, :8]]
    unnamed x11 -> x13, local copies, waits for them, and re-layouts: 3.45 us -> 4.45 us
    pallas_call x1 -> x2, Pallas kernels: 24.1 us -> 23.5 us  [the longest x1 23.4 us: chain(): pl.pallas_call(functools.partial(chain_kernel, tuple(SPLITS), PIECE, ROLL...]
  transfers between devices with their start and end apart: 3 -> 3, of which waited for: 2 -> 1; matrix products, arithmetic and copies ran while one was open for 1% -> 1% of each run, Pallas kernels for 1% -> 1%
where the time goes in v3:
time: 102 us
  blocking collectives  35.2 us (35%)
  Pallas kernels  31.2 us (31%)
  starting transfers between devices  18.8 us (18%)
  waiting for transfers between devices  12.1 us (12%)
  local copies, waits for them, and re-layouts  4.45 us (4%)
    pallas_call x1, Pallas kernels, chain(): pl.pallas_call(functools.partial(chain_kernel, tuple(SPLITS), PIECE, ROLL...  23.4 us
    all_to_all x1, blocking collectives, shards(): recv = lax.all_to_all(send, 'tm', 0, 0)  22.6 us
    all_to_all x1, starting transfers between devices, shards(): c = lax.all_to_all(c, 'space', 0, 0)  13.1 us
    all_to_all x1, blocking collectives, shards(): g = lax.all_to_all(g, 'tm', 0, 0)  12.5 us
    all_to_all x1, waiting for transfers between devices, shards(): c = lax.all_to_all(c, 'space', 0, 0)  12.1 us
    pallas_call x1, Pallas kernels, shards(): pl.pallas_call(first_kernel, out_shape=[jax.ShapeDtypeStruct(slab.shape,...  4.59 us
    unnamed x13, local copies, waits for them, and re-layouts  4.45 us
    ppermute x1, starting transfers between devices, shards(): lax.ppermute(down, 'space', [((i + 1) % count, i) for i in range(count)])  3.64 us
  transfers between devices with their start and end apart: 3, of which 1 were waited for; matrix products, arithmetic and copies ran while one was open for 1% of the time, Pallas kernels for 1%

profile of v3, /device:TPU:2, one launch (start us, length us, event | category | flops | bytes accessed | tf_op | source)
XLA Modules:
  0.0 101.8 jit_solution(8378437604838370482)
XLA Ops:
  0.0 0.0 copy-start
  0.0 1.0 copy-done
  1.0 0.0 copy-start.1
  1.0 0.0 copy-start.3
  1.0 0.1 edges.1
  1.1 2.1 %collective-permute-start = (f32[4,4,2048]{2,1,0:T(4,128)S(1)}, f32[4,4,2048]{2,1,0:T(4,128)S(1)}, u32[]{:S(2)}, u32[]{:S(2)}) collective-permute-start(f32[4,4,2048]{2,1,0:T(4,128)S(1)} %get-tuple-element.12), channel_id=1, source_target_pairs={{0,1},{1,2},{2,3},{3,4},{4,5},{5,6},{6,7},{7,8},{8,9},{9,10},{10,1... | collective-permute-start | bytes 393224 | tf_op jit(solution)/shard_map/ppermute | solution.py:360
  3.2 3.6 %collective-permute-start.1 = (f32[4,4,2048]{2,1,0:T(4,128)S(1)}, f32[4,4,2048]{2,1,0:T(4,128)S(1)}, u32[]{:S(2)}, u32[]{:S(2)}) collective-permute-start(f32[4,4,2048]{2,1,0:T(4,128)S(1)} %get-tuple-element.13), channel_id=1, source_target_pairs={{1,0},{2,1},{3,2},{4,3},{5,4},{6,5},{7,6},{8,7},{9,8},{10,9},{11,1... | collective-permute-start | bytes 393224 | tf_op jit(solution)/shard_map/ppermute | solution.py:361
  6.8 0.8 copy.7.lwt_ref
  7.6 0.0 copy-start.2
  7.7 1.3 %copy-done.2 = bf16[3,3,256,256]{3,2,1,0:T(8,128)(2,1)S(1)} copy-done((bf16[3,3,256,256]{3,2,1,0:T(8,128)(2,1)S(1)}, bf16[3,3,256,256]{3,2,1,0:T(8,128)(2,1)}, u32[]{:S(2)}) %copy-start.2) | copy-done | bytes 1179672
  8.9 0.0 copy-start.4
  8.9 0.7 copy-done.4
  9.6 0.0 copy-start.5
  9.6 0.7 copy-done.5
  10.3 0.6 tables.1
  10.9 0.0 collective-permute-done.up_ref
  10.9 0.0 collective-permute-done.1.dn_ref
  10.9 0.0 copy-done.1
  10.9 0.0 copy-done.3
  10.9 4.6 %fine_and_guess.1 = (f32[3,16,2048]{2,1,0:T(8,128)S(1)}, f32[32,8,256]{2,1,0:T(8,128)}) custom-call(s32[1]{0:T(128)} %bitcast.1.tm_ref, f32[1,3,16,2048]{3,2,1,0:T(8,128)S(1)} %copy-done.1, f32[4,4,2048]{2,1,0:T(4,128)S(1)} %collective-permute-done.up_ref, f32[4,4,2048]{2,1,0:T(4,128)S(1)} %collective-permute-done.1.dn_ref, ...), custom_call_target="tpu_custom_call" | custom-call | tf_op jit(solution)/shard_map/fine_and_guess/pallas_call | solution.py:365
  15.5 13.1 %all-to-all-start = ((f32[32,8,256]{2,1,0:T(8,128)}), f32[32,8,256]{2,1,0:T(8,128)S(1)}, u32[]{:S(2)}, u32[]{:S(2)}) async-start(f32[32,8,256]{2,1,0:T(8,128)} %get-tuple-element.17), calls=%async_computation | async-start | bytes 524288 | tf_op jit(solution)/shard_map/all_to_all | solution.py:372
  28.6 12.1 %all-to-all-done.b_ref = f32[32,8,256]{2,1,0:T(8,128)S(1)} async-done(((f32[32,8,256]{2,1,0:T(8,128)}), f32[32,8,256]{2,1,0:T(8,128)S(1)}, u32[]{:S(2)}, u32[]{:S(2)}) %all-to-all-start) | async-done | bytes 262176 | tf_op jit(solution)/shard_map/all_to_all | solution.py:372
  40.7 1.6 %windows.1 = f32[16,4,1152]{2,1,0:T(4,128)S(1)} custom-call(s32[1]{0:T(128)} %bitcast.sp_ref, f32[32,8,256]{2,1,0:T(8,128)S(1)} %all-to-all-done.b_ref), custom_call_target="tpu_custom_call" | custom-call | tf_op jit(solution)/shard_map/windows/pallas_call | solution.py:373
  42.3 22.6 %all_to_all.15.r_ref = f32[16,4,1152]{2,1,0:T(4,128)S(1)} all-to-all(f32[16,4,1152]{2,1,0:T(4,128)S(1)} %windows.1), channel_id=1, replica_groups=mesh['tm'=16,'space'=32] {'tm'}, dimensions={0} | all-to-all | bytes 589824 | tf_op jit(solution)/shard_map/all_to_all | solution.py:378
  64.9 23.4 %shard_map.64 = f32[16,1,128]{2,1,0:T(1,128)S(1)} custom-call(f32[16,4,1152]{2,1,0:T(4,128)S(1)} %all_to_all.15.r_ref, bf16[3,768,256]{2,1,0:T(8,128)(2,1)S(1)} %get-tuple-element.14.wt_ref, bf16[256,256]{1,0:T(8,128)(2,1)S(1)} %get-tuple-element.15.lw_ref, bf16[256,128]{1,0:T(8,128)(2,1)S(1)} %get-tuple-element.16.ow_ref, f32[1,256]{1,0:T(1,128)S(1)} %bitcast.5), custom_call_target="tpu_custom_call" | custom-call | tf_op jit(solution)/shard_map/pallas_call | solution.py:183
  88.3 12.5 %all_to_all.16.g_ref = f32[16,1,128]{2,1,0:T(1,128)S(1)} all-to-all(f32[16,1,128]{2,1,0:T(1,128)S(1)} %shard_map.64), channel_id=1, replica_groups=mesh['tm'=16,'space'=32] {'tm'}, dimensions={0} | all-to-all | bytes 16384 | tf_op jit(solution)/shard_map/all_to_all | solution.py:380
  100.9 1.0 correct.1
Async XLA Ops:
  0.0 1.0 copy-start
  1.0 9.9 %copy-start.1 = (f32[1,3,16,2048]{3,2,1,0:T(8,128)S(1)}, f32[1,3,16,2048]{3,2,1,0:T(8,128)}, u32[]{:S(2)}) copy-start(f32[1,3,16,2048]{3,2,1,0:T(8,128)} %s_ref.3) | copy-start | bytes 1179652
  1.0 9.9 %copy-start.3 = (f32[256]{0:T(256)S(1)}, f32[256]{0:T(256)}, u32[]{:S(2)}) copy-start(f32[256]{0:T(256)} %param.10) | copy-start | bytes 3076
  1.1 9.8 %collective-permute-start = (f32[4,4,2048]{2,1,0:T(4,128)S(1)}, f32[4,4,2048]{2,1,0:T(4,128)S(1)}, u32[]{:S(2)}, u32[]{:S(2)}) collective-permute-start(f32[4,4,2048]{2,1,0:T(4,128)S(1)} %get-tuple-element.12), channel_id=1, source_target_pairs={{0,1},{1,2},{2,3},{3,4},{4,5},{5,6},{6,7},{7,8},{8,9},{9,10},{10,1... | collective-permute-start | bytes 393224 | tf_op jit(solution)/shard_map/ppermute | solution.py:360
  3.2 7.7 %collective-permute-start.1 = (f32[4,4,2048]{2,1,0:T(4,128)S(1)}, f32[4,4,2048]{2,1,0:T(4,128)S(1)}, u32[]{:S(2)}, u32[]{:S(2)}) collective-permute-start(f32[4,4,2048]{2,1,0:T(4,128)S(1)} %get-tuple-element.13), channel_id=1, source_target_pairs={{1,0},{2,1},{3,2},{4,3},{5,4},{6,5},{7,6},{8,7},{9,8},{10,9},{11,1... | collective-permute-start | bytes 393224 | tf_op jit(solution)/shard_map/ppermute | solution.py:361
  7.6 1.3 %copy-start.2 = (bf16[3,3,256,256]{3,2,1,0:T(8,128)(2,1)S(1)}, bf16[3,3,256,256]{3,2,1,0:T(8,128)(2,1)}, u32[]{:S(2)}) copy-start(bf16[3,3,256,256]{3,2,1,0:T(8,128)(2,1)} %cw_ref.1) | copy-start | bytes 3538948
  8.9 0.7 copy-start.4
  9.6 0.7 copy-start.5
  15.5 25.2 %all-to-all-start = ((f32[32,8,256]{2,1,0:T(8,128)}), f32[32,8,256]{2,1,0:T(8,128)S(1)}, u32[]{:S(2)}, u32[]{:S(2)}) async-start(f32[32,8,256]{2,1,0:T(8,128)} %get-tuple-element.17), calls=%async_computation | async-start | bytes 524288 | tf_op jit(solution)/shard_map/all_to_all | solution.py:372

commit v4 on v3

--- a/solution.py
+++ b/solution.py
@@ -189,17 +189,16 @@
         compiler_params=pltpu.CompilerParams(vmem_limit_bytes=48 * 2**20),
     )(recv, wt, lw, ow, cb)
 
-def table_kernel(lwt_ref, lb_ref, cw_ref, ow_ref, wt_ref, lw_ref, owr_ref, wide_ref, rows_ref):
+def table_kernel(cw_ref, small_ref, wt_ref, lw_ref, owr_ref, rows_ref):
     for i in range(3):
         for j in range(3):
             wt_ref[i, 256 * j:256 * j + 256, :] = (0.5 * cw_ref[i, j].astype(f32)).T.astype(bf16)
-    wide_ref[...] = jnp.zeros(wide_ref.shape, f32)
-    wide_ref[:, 0:3] = lwt_ref[...]
-    w = wide_ref[...].T[0:8]
+    rows_ref[...] = jnp.zeros(rows_ref.shape, f32)
+    w = small_ref[0:3, :]
     hi = w.astype(bf16).astype(f32)
-    rows_ref[0:8, :] = hi
-    rows_ref[8:16, :] = w - hi
-    b = lb_ref[...]
+    rows_ref[0:3, :] = hi
+    rows_ref[8:11, :] = w - hi
+    b = small_ref[3:4, :]
     bhi = b.astype(bf16).astype(f32)
     rows_ref[3:4, :] = bhi
     rows_ref[11:12, :] = b - bhi
@@ -211,7 +210,7 @@
     pick = jnp.where(weight | bias, 1.0, 0.0).astype(bf16)
     lw_ref[...] = jnp.dot(pick, rows_ref[...].astype(bf16), preferred_element_type=f32).astype(bf16)
     rows_ref[...] = jnp.zeros(rows_ref.shape, f32)
-    rows_ref[0:3, :] = 0.5 * ow_ref[...].astype(f32)
+    rows_ref[0:3, :] = 0.5 * small_ref[4:7, :]
     lane = lax.broadcasted_iota(jnp.int32, (128, 16), 0) & 3
     pick = jnp.where((lane < 3) & (lane == lax.broadcasted_iota(jnp.int32, (128, 16), 1)), 1.0, 0.0).astype(bf16)
     owr_ref[...] = jnp.dot(pick, rows_ref[...].astype(bf16), preferred_element_type=f32).T.astype(bf16)
@@ -221,11 +220,11 @@
     wt, lw, ow = pl.pallas_call(
         table_kernel,
         out_shape=[jax.ShapeDtypeStruct((3, 768, 256), bf16), jax.ShapeDtypeStruct((256, 256), bf16), jax.ShapeDtypeStruct((256, 128), bf16)],
-        in_specs=[vm] * 4, out_specs=[vm] * 3,
-        scratch_shapes=[pltpu.VMEM((256, 128), f32), pltpu.VMEM((16, 256), f32)],
+        in_specs=[vm] * 2, out_specs=[vm] * 3,
+        scratch_shapes=[pltpu.VMEM((16, 256), f32)],
         compiler_params=pltpu.CompilerParams(vmem_limit_bytes=32 * 2**20),
         cost_estimate=pl.CostEstimate(flops=10**7, bytes_accessed=10**7, transcendentals=0), name="tables",
-    )(lift_weight, lift_bias[None], conv_weight, out_weight)
+    )(conv_weight, jnp.concatenate([lift_weight.T, lift_bias[None], out_weight.astype(f32)], axis=0))
     return wt, lw, ow, conv_bias[None]
 
 def thirds(x):

time: 102 us -> 102 us (level)
  local copies, waits for them, and re-layouts: 4.45 us -> 2.27 us
  other arithmetic: 0 us -> 1.4 us
    unnamed x13 -> x8, local copies, waits for them, and re-layouts: 4.45 us -> 2.27 us
  transfers between devices with their start and end apart: 3 -> 3, of which waited for: 1 -> 1; matrix products, arithmetic and copies ran while one was open for 1% -> 1% of each run, Pallas kernels for 1% -> 0%
where the time goes in v4:
time: 102 us
  blocking collectives  35.2 us (35%)
  Pallas kernels  31.1 us (30%)
  starting transfers between devices  19.4 us (19%)
  waiting for transfers between devices  12.1 us (12%)
  local copies, waits for them, and re-layouts  2.27 us (2%)
  other arithmetic  1.4 us (1%)
    pallas_call x1, Pallas kernels, chain(): pl.pallas_call(functools.partial(chain_kernel, tuple(SPLITS), PIECE, ROLL...  23.4 us
    all_to_all x1, blocking collectives, shards(): recv = lax.all_to_all(send, 'tm', 0, 0)  22.6 us
    all_to_all x1, starting transfers between devices, shards(): c = lax.all_to_all(c, 'space', 0, 0)  13.7 us
    all_to_all x1, blocking collectives, shards(): g = lax.all_to_all(g, 'tm', 0, 0)  12.5 us
    all_to_all x1, waiting for transfers between devices, shards(): c = lax.all_to_all(c, 'space', 0, 0)  12.1 us
    pallas_call x1, Pallas kernels, shards(): pl.pallas_call(first_kernel, out_shape=[jax.ShapeDtypeStruct(slab.shape,...  4.6 us
    ppermute x1, starting transfers between devices, shards(): lax.ppermute(down, 'space', [((i + 1) % count, i) for i in range(count)])  3.64 us
    unnamed x8, local copies, waits for them, and re-layouts  2.27 us
  transfers between devices with their start and end apart: 3, of which 1 were waited for; matrix products, arithmetic and copies ran while one was open for 1% of the time, Pallas kernels for 0%

profile of v4, /device:TPU:2, one launch (start us, length us, event | category | flops | bytes accessed | tf_op | source)
XLA Modules:
  0.0 101.5 jit_solution(16361926351684883465)
XLA Ops:
  0.0 0.0 copy-start
  0.0 1.0 copy-done
  1.0 0.0 copy-start.1
  1.0 0.0 copy-start.3
  1.0 0.1 edges.1
  1.1 2.1 %collective-permute-start = (f32[4,4,2048]{2,1,0:T(4,128)S(1)}, f32[4,4,2048]{2,1,0:T(4,128)S(1)}, u32[]{:S(2)}, u32[]{:S(2)}) collective-permute-start(f32[4,4,2048]{2,1,0:T(4,128)S(1)} %get-tuple-element.12), channel_id=1, source_target_pairs={{0,1},{1,2},{2,3},{3,4},{4,5},{5,6},{6,7},{7,8},{8,9},{9,10},{10,1... | collective-permute-start | bytes 393224 | tf_op jit(solution)/shard_map/ppermute | solution.py:359
  3.2 3.6 %collective-permute-start.1 = (f32[4,4,2048]{2,1,0:T(4,128)S(1)}, f32[4,4,2048]{2,1,0:T(4,128)S(1)}, u32[]{:S(2)}, u32[]{:S(2)}) collective-permute-start(f32[4,4,2048]{2,1,0:T(4,128)S(1)} %get-tuple-element.13), channel_id=1, source_target_pairs={{1,0},{2,1},{3,2},{4,3},{5,4},{6,5},{7,6},{8,7},{9,8},{10,9},{11,1... | collective-permute-start | bytes 393224 | tf_op jit(solution)/shard_map/ppermute | solution.py:360
  6.8 0.7 convert_element_type.3
  7.5 0.7 pad_maximum_fusion.small_ref
  8.2 0.0 copy-start.2
  8.2 1.3 %copy-done.2 = bf16[3,3,256,256]{3,2,1,0:T(8,128)(2,1)S(1)} copy-done((bf16[3,3,256,256]{3,2,1,0:T(8,128)(2,1)S(1)}, bf16[3,3,256,256]{3,2,1,0:T(8,128)(2,1)}, u32[]{:S(2)}) %copy-start.2) | copy-done | bytes 1179672
  9.5 0.5 tables.1
  10.0 0.0 collective-permute-done.up_ref
  10.0 0.0 collective-permute-done.1.dn_ref
  10.0 0.0 copy-done.1
  10.0 0.0 copy-done.3
  10.0 4.6 %fine_and_guess.1 = (f32[3,16,2048]{2,1,0:T(8,128)S(1)}, f32[32,8,256]{2,1,0:T(8,128)}) custom-call(s32[1]{0:T(128)} %bitcast.1.tm_ref, f32[1,3,16,2048]{3,2,1,0:T(8,128)S(1)} %copy-done.1, f32[4,4,2048]{2,1,0:T(4,128)S(1)} %collective-permute-done.up_ref, f32[4,4,2048]{2,1,0:T(4,128)S(1)} %collective-permute-done.1.dn_ref, ...), custom_call_target="tpu_custom_call" | custom-call | tf_op jit(solution)/shard_map/fine_and_guess/pallas_call | solution.py:364
  14.6 13.7 %all-to-all-start = ((f32[32,8,256]{2,1,0:T(8,128)}), f32[32,8,256]{2,1,0:T(8,128)S(1)}, u32[]{:S(2)}, u32[]{:S(2)}) async-start(f32[32,8,256]{2,1,0:T(8,128)} %get-tuple-element.17), calls=%async_computation | async-start | bytes 524288 | tf_op jit(solution)/shard_map/all_to_all | solution.py:371
  28.3 12.1 %all-to-all-done.b_ref = f32[32,8,256]{2,1,0:T(8,128)S(1)} async-done(((f32[32,8,256]{2,1,0:T(8,128)}), f32[32,8,256]{2,1,0:T(8,128)S(1)}, u32[]{:S(2)}, u32[]{:S(2)}) %all-to-all-start) | async-done | bytes 262176 | tf_op jit(solution)/shard_map/all_to_all | solution.py:371
  40.4 1.6 %windows.1 = f32[16,4,1152]{2,1,0:T(4,128)S(1)} custom-call(s32[1]{0:T(128)} %bitcast.sp_ref, f32[32,8,256]{2,1,0:T(8,128)S(1)} %all-to-all-done.b_ref), custom_call_target="tpu_custom_call" | custom-call | tf_op jit(solution)/shard_map/windows/pallas_call | solution.py:372
  42.0 22.6 %all_to_all.15.r_ref = f32[16,4,1152]{2,1,0:T(4,128)S(1)} all-to-all(f32[16,4,1152]{2,1,0:T(4,128)S(1)} %windows.1), channel_id=1, replica_groups=mesh['tm'=16,'space'=32] {'tm'}, dimensions={0} | all-to-all | bytes 589824 | tf_op jit(solution)/shard_map/all_to_all | solution.py:377
  64.6 23.4 %shard_map.64 = f32[16,1,128]{2,1,0:T(1,128)S(1)} custom-call(f32[16,4,1152]{2,1,0:T(4,128)S(1)} %all_to_all.15.r_ref, bf16[3,768,256]{2,1,0:T(8,128)(2,1)S(1)} %get-tuple-element.14.wt_ref, bf16[256,256]{1,0:T(8,128)(2,1)S(1)} %get-tuple-element.15.lw_ref, bf16[256,128]{1,0:T(8,128)(2,1)S(1)} %get-tuple-element.16.ow_ref, f32[1,256]{1,0:T(1,128)S(1)} %bitcast.6), custom_call_target="tpu_custom_call" | custom-call | tf_op jit(solution)/shard_map/pallas_call | solution.py:183
  88.0 12.5 %all_to_all.16.g_ref = f32[16,1,128]{2,1,0:T(1,128)S(1)} all-to-all(f32[16,1,128]{2,1,0:T(1,128)S(1)} %shard_map.64), channel_id=1, replica_groups=mesh['tm'=16,'space'=32] {'tm'}, dimensions={0} | all-to-all | bytes 16384 | tf_op jit(solution)/shard_map/all_to_all | solution.py:379
  100.6 1.0 correct.1
Async XLA Ops:
  0.0 1.0 copy-start
  1.0 9.0 %copy-start.1 = (f32[1,3,16,2048]{3,2,1,0:T(8,128)S(1)}, f32[1,3,16,2048]{3,2,1,0:T(8,128)}, u32[]{:S(2)}) copy-start(f32[1,3,16,2048]{3,2,1,0:T(8,128)} %s_ref.3) | copy-start | bytes 1179652
  1.0 9.0 %copy-start.3 = (f32[256]{0:T(256)S(1)}, f32[256]{0:T(256)}, u32[]{:S(2)}) copy-start(f32[256]{0:T(256)} %param.10) | copy-start | bytes 3076
  1.1 8.9 %collective-permute-start = (f32[4,4,2048]{2,1,0:T(4,128)S(1)}, f32[4,4,2048]{2,1,0:T(4,128)S(1)}, u32[]{:S(2)}, u32[]{:S(2)}) collective-permute-start(f32[4,4,2048]{2,1,0:T(4,128)S(1)} %get-tuple-element.12), channel_id=1, source_target_pairs={{0,1},{1,2},{2,3},{3,4},{4,5},{5,6},{6,7},{7,8},{8,9},{9,10},{10,1... | collective-permute-start | bytes 393224 | tf_op jit(solution)/shard_map/ppermute | solution.py:359
  3.2 6.8 %collective-permute-start.1 = (f32[4,4,2048]{2,1,0:T(4,128)S(1)}, f32[4,4,2048]{2,1,0:T(4,128)S(1)}, u32[]{:S(2)}, u32[]{:S(2)}) collective-permute-start(f32[4,4,2048]{2,1,0:T(4,128)S(1)} %get-tuple-element.13), channel_id=1, source_target_pairs={{1,0},{2,1},{3,2},{4,3},{5,4},{6,5},{7,6},{8,7},{9,8},{10,9},{11,1... | collective-permute-start | bytes 393224 | tf_op jit(solution)/shard_map/ppermute | solution.py:360
  8.2 1.3 %copy-start.2 = (bf16[3,3,256,256]{3,2,1,0:T(8,128)(2,1)S(1)}, bf16[3,3,256,256]{3,2,1,0:T(8,128)(2,1)}, u32[]{:S(2)}) copy-start(bf16[3,3,256,256]{3,2,1,0:T(8,128)(2,1)} %cw_ref.1) | copy-start | bytes 3538948
  14.6 25.8 %all-to-all-start = ((f32[32,8,256]{2,1,0:T(8,128)}), f32[32,8,256]{2,1,0:T(8,128)S(1)}, u32[]{:S(2)}, u32[]{:S(2)}) async-start(f32[32,8,256]{2,1,0:T(8,128)} %get-tuple-element.17), calls=%async_computation | async-start | bytes 524288 | tf_op jit(solution)/shard_map/all_to_all | solution.py:371

commit v5 on v4

--- a/solution.py
+++ b/solution.py
@@ -262,7 +262,7 @@
         down_ref[f] = s_ref[0, f, 0:4, :]
         down_ref[3, f:f + 1, :] = jnp.sum(s_ref[0, f, 0:8, :], axis=0, keepdims=True)
 
-def first_kernel(tm_ref, s_ref, up_ref, dn_ref, wt_ref, lw_ref, ow_ref, cb_ref, corr_ref, c_ref, q_ref, qf_ref, h_ref):
+def first_kernel(tm_ref, s_ref, up_ref, dn_ref, wt_ref, lw_ref, ow_ref, cb_ref, fine_ref, delta_ref, c_ref, q_ref, qf_ref, h_ref):
     blank = jnp.zeros((4, s_ref.shape[3]), f32)
     fields = [jnp.concatenate([blank, up_ref[f], s_ref[0, f], dn_ref[f], blank], axis=0) for f in range(3)]
     q_ref[...] = jnp.zeros(q_ref.shape, f32)
@@ -274,7 +274,6 @@
             q_ref[4 + 4 * r + f:5 + 4 * r + f, :] = jnp.sum(s_ref[0, f, 8 * r:8 * r + 8, :], axis=0, keepdims=True)
     half = 128 * RF
     pool = (lax.broadcasted_iota(jnp.int32, (half, 128), 0) // RF == lax.broadcasted_iota(jnp.int32, (half, 128), 1)).astype(f32).astype(bf16)
-    spread = (lax.broadcasted_iota(jnp.int32, (128, half), 1) // RF == lax.broadcasted_iota(jnp.int32, (128, half), 0)).astype(f32).astype(bf16)
 
     def pooled(ref):
         return jnp.concatenate([exact_dot(ref[:, 0:half], pool), exact_dot(ref[:, half:], pool)], axis=1) * (1.0 / (RF * RF))
@@ -311,12 +310,19 @@
     c = first + (pooled(qf_ref) - guess)
     for i in range(c_ref.shape[0]):
         c_ref[i] = c
-    delta = guess - first
+    delta_ref[...] = guess - first
+    for f in range(3):
+        fine_ref[f] = fields[f][8:24]
+
+def subtract_kernel(fine_ref, delta_ref, corr_ref):
+    half = 128 * RF
+    spread = (lax.broadcasted_iota(jnp.int32, (128, half), 1) // RF == lax.broadcasted_iota(jnp.int32, (128, half), 0)).astype(f32).astype(bf16)
     for p in range(2):
-        wide = exact_dot(delta[:, 128 * p:128 * p + 128], spread)
+        wide = exact_dot(delta_ref[:, 128 * p:128 * p + 128], spread)
         for f in range(3):
             for r in range(2):
-                corr_ref[f, 8 * r:8 * r + 8, half * p:half * p + half] = fields[f][8 + 8 * r:16 + 8 * r, half * p:half * p + half] - wide[4 * r + f:4 * r + f + 1]
+                at = pl.ds(half * p, half)
+                corr_ref[f, 8 * r:8 * r + 8, at] = fine_ref[f, 8 * r:8 * r + 8, at] - wide[4 * r + f:4 * r + f + 1]
 
 def window_kernel(sp_ref, b_ref, out_ref, w_ref):
     count = b_ref.shape[0]
@@ -361,14 +367,18 @@
     weights = tables(lift_weight, lift_bias, conv_weight, conv_bias, out_weight)
     tm = lax.axis_index("tm").astype(jnp.int32).reshape(1)
     sp = lax.axis_index("space").astype(jnp.int32).reshape(1)
-    corr, c = pl.pallas_call(
+    fine, delta, c = pl.pallas_call(
         first_kernel,
-        out_shape=[jax.ShapeDtypeStruct(slab.shape, f32), jax.ShapeDtypeStruct((count, 8, 256), f32)],
-        in_specs=[sm] + [vm] * 7, out_specs=[vm, vm],
+        out_shape=[jax.ShapeDtypeStruct(slab.shape, f32), jax.ShapeDtypeStruct((8, 256), f32), jax.ShapeDtypeStruct((count, 8, 256), f32)],
+        in_specs=[sm] + [vm] * 7, out_specs=[vm] * 3,
         scratch_shapes=[pltpu.VMEM((16, slab.shape[2]), f32), pltpu.VMEM((8, slab.shape[2]), f32), pltpu.VMEM((1024, 768), bf16)],
         compiler_params=params, name="fine_and_guess",
     )(tm, start_states, up, down, *weights)
     c = lax.all_to_all(c, "space", 0, 0)
+    corr = pl.pallas_call(
+        subtract_kernel, out_shape=jax.ShapeDtypeStruct(slab.shape, f32), in_specs=[vm, vm], out_specs=vm, compiler_params=params,
+        cost_estimate=pl.CostEstimate(flops=10**6, bytes_accessed=10**6, transcendentals=0), name="subtract",
+    )(fine, delta)
     send = pl.pallas_call(
         window_kernel, out_shape=jax.ShapeDtypeStruct((N, 4, 3 * ROWS * W1 // 4), f32),
         in_specs=[sm, vm], out_specs=vm, scratch_shapes=[pltpu.VMEM((24, 4, 256), f32)],

time: 102 us -> 103 us (level)
  blocking collectives: 35.2 us -> 22.6 us
  waiting for transfers between devices: 12.1 us -> 21.8 us
  starting transfers between devices: 19.4 us -> 22.9 us
    all_to_all x1 -> x0, blocking collectives: 12.5 us -> none  [shards(): g = lax.all_to_all(g, 'tm', 0, 0)]
    all_to_all x0 -> x1, waiting for transfers between devices: none -> 9.66 us  [shards(): g = lax.all_to_all(g, 'tm', 0, 0)]
    all_to_all x0 -> x1, starting transfers between devices: none -> 3.47 us  [shards(): g = lax.all_to_all(g, 'tm', 0, 0)]
  transfers between devices with their start and end apart: 3 -> 4, of which waited for: 1 -> 2; matrix products, arithmetic and copies ran while one was open for 1% -> 1% of each run, Pallas kernels for 0% -> 1%
where the time goes in v5:
time: 103 us
  Pallas kernels  31.9 us (31%)
  starting transfers between devices  22.9 us (22%)
  blocking collectives  22.6 us (22%)
  waiting for transfers between devices  21.8 us (21%)
  local copies, waits for them, and re-layouts  2.27 us (2%)
  other arithmetic  1.4 us (1%)
    pallas_call x1, Pallas kernels, chain(): pl.pallas_call(functools.partial(chain_kernel, tuple(SPLITS), PIECE, ROLL...  24 us
    all_to_all x1, blocking collectives, shards(): recv = lax.all_to_all(send, 'tm', 0, 0)  22.6 us
    all_to_all x1, starting transfers between devices, shards(): c = lax.all_to_all(c, 'space', 0, 0)  13.7 us
    all_to_all x1, waiting for transfers between devices, shards(): c = lax.all_to_all(c, 'space', 0, 0)  12.1 us
    all_to_all x1, waiting for transfers between devices, shards(): g = lax.all_to_all(g, 'tm', 0, 0)  9.66 us
    pallas_call x1, Pallas kernels, shards(): pl.pallas_call(first_kernel, out_shape=[jax.ShapeDtypeStruct(slab.shape,...  4.58 us
    ppermute x1, starting transfers between devices, shards(): lax.ppermute(down, 'space', [((i + 1) % count, i) for i in range(count)])  3.64 us
    all_to_all x1, starting transfers between devices, shards(): g = lax.all_to_all(g, 'tm', 0, 0)  3.47 us
  transfers between devices with their start and end apart: 4, of which 2 were waited for; matrix products, arithmetic and copies ran while one was open for 1% of the time, Pallas kernels for 1%

profile of v5, /device:TPU:2, one launch (start us, length us, event | category | flops | bytes accessed | tf_op | source)
XLA Modules:
  0.0 102.9 jit_solution(6373120032384740918)
XLA Ops:
  0.0 0.0 copy-start
  0.0 1.0 copy-done
  1.0 0.0 copy-start.1
  1.0 0.0 copy-start.3
  1.0 0.1 edges.1
  1.1 2.1 %collective-permute-start = (f32[4,4,2048]{2,1,0:T(4,128)S(1)}, f32[4,4,2048]{2,1,0:T(4,128)S(1)}, u32[]{:S(2)}, u32[]{:S(2)}) collective-permute-start(f32[4,4,2048]{2,1,0:T(4,128)S(1)} %get-tuple-element.13), channel_id=1, source_target_pairs={{0,1},{1,2},{2,3},{3,4},{4,5},{5,6},{6,7},{7,8},{8,9},{9,10},{10,1... | collective-permute-start | bytes 393224 | tf_op jit(solution)/shard_map/ppermute | solution.py:365
  3.2 3.6 %collective-permute-start.1 = (f32[4,4,2048]{2,1,0:T(4,128)S(1)}, f32[4,4,2048]{2,1,0:T(4,128)S(1)}, u32[]{:S(2)}, u32[]{:S(2)}) collective-permute-start(f32[4,4,2048]{2,1,0:T(4,128)S(1)} %get-tuple-element.14), channel_id=1, source_target_pairs={{1,0},{2,1},{3,2},{4,3},{5,4},{6,5},{7,6},{8,7},{9,8},{10,9},{11,1... | collective-permute-start | bytes 393224 | tf_op jit(solution)/shard_map/ppermute | solution.py:366
  6.8 0.7 convert_element_type.3
  7.5 0.7 pad_maximum_fusion.small_ref
  8.2 0.0 copy-start.2
  8.2 1.3 %copy-done.2 = bf16[3,3,256,256]{3,2,1,0:T(8,128)(2,1)S(1)} copy-done((bf16[3,3,256,256]{3,2,1,0:T(8,128)(2,1)S(1)}, bf16[3,3,256,256]{3,2,1,0:T(8,128)(2,1)}, u32[]{:S(2)}) %copy-start.2) | copy-done | bytes 1179672
  9.5 0.5 tables.1
  10.0 0.0 collective-permute-done.up_ref
  10.0 0.0 collective-permute-done.1.dn_ref
  10.0 0.0 copy-done.1
  10.0 0.0 copy-done.3
  10.0 4.6 %fine_and_guess.1 = (f32[3,16,2048]{2,1,0:T(8,128)S(1)}, f32[8,256]{1,0:T(8,128)S(1)}, f32[32,8,256]{2,1,0:T(8,128)}) custom-call(s32[1]{0:T(128)} %bitcast.1.tm_ref, f32[1,3,16,2048]{3,2,1,0:T(8,128)S(1)} %copy-done.1, f32[4,4,2048]{2,1,0:T(4,128)S(1)} %collective-permute-done.up_ref, f32[4,4,2048]{2,1,0:T(4,128)S(1)} %collective-permute-done.1.dn_ref, ...), custom_call_target="tpu_custom_call" | custom-call | tf_op jit(solution)/shard_map/fine_and_guess/pallas_call | solution.py:370
  14.6 13.7 %all-to-all-start = ((f32[32,8,256]{2,1,0:T(8,128)}), f32[32,8,256]{2,1,0:T(8,128)S(1)}, u32[]{:S(2)}, u32[]{:S(2)}) async-start(f32[32,8,256]{2,1,0:T(8,128)} %get-tuple-element.18), calls=%async_computation | async-start | bytes 524288 | tf_op jit(solution)/shard_map/all_to_all | solution.py:377
  28.3 12.1 %all-to-all-done.b_ref = f32[32,8,256]{2,1,0:T(8,128)S(1)} async-done(((f32[32,8,256]{2,1,0:T(8,128)}), f32[32,8,256]{2,1,0:T(8,128)S(1)}, u32[]{:S(2)}, u32[]{:S(2)}) %all-to-all-start) | async-done | bytes 262176 | tf_op jit(solution)/shard_map/all_to_all | solution.py:377
  40.4 1.6 %windows.1 = f32[16,4,1152]{2,1,0:T(4,128)S(1)} custom-call(s32[1]{0:T(128)} %bitcast.sp_ref, f32[32,8,256]{2,1,0:T(8,128)S(1)} %all-to-all-done.b_ref), custom_call_target="tpu_custom_call" | custom-call | tf_op jit(solution)/shard_map/windows/pallas_call | solution.py:382
  42.0 22.6 %all_to_all.15.r_ref = f32[16,4,1152]{2,1,0:T(4,128)S(1)} all-to-all(f32[16,4,1152]{2,1,0:T(4,128)S(1)} %windows.1), channel_id=1, replica_groups=mesh['tm'=16,'space'=32] {'tm'}, dimensions={0} | all-to-all | bytes 589824 | tf_op jit(solution)/shard_map/all_to_all | solution.py:387
  64.6 24.0 %shard_map.64 = f32[16,1,128]{2,1,0:T(1,128)} custom-call(f32[16,4,1152]{2,1,0:T(4,128)S(1)} %all_to_all.15.r_ref, bf16[3,768,256]{2,1,0:T(8,128)(2,1)S(1)} %get-tuple-element.15.wt_ref, bf16[256,256]{1,0:T(8,128)(2,1)S(1)} %get-tuple-element.16.lw_ref, bf16[256,128]{1,0:T(8,128)(2,1)S(1)} %get-tuple-element.17.ow_ref, f32[1,256]{1,0:T(1,128)S(1)} %bitcast.6), custom_call_target="tpu_custom_call" | custom-call | tf_op jit(solution)/shard_map/pallas_call | solution.py:183
  88.6 3.5 %all-to-all-start.2 = ((f32[16,1,128]{2,1,0:T(1,128)}), f32[16,1,128]{2,1,0:T(1,128)S(1)}, u32[]{:S(2)}, u32[]{:S(2)}) async-start(f32[16,1,128]{2,1,0:T(1,128)} %shard_map.64), calls=%async_computation.2 | async-start | bytes 16384 | tf_op jit(solution)/shard_map/all_to_all | solution.py:389
  92.1 0.2 subtract.1.corr_ref
  92.3 9.7 %all-to-all-done.2.g_ref = f32[16,1,128]{2,1,0:T(1,128)S(1)} async-done(((f32[16,1,128]{2,1,0:T(1,128)}), f32[16,1,128]{2,1,0:T(1,128)S(1)}, u32[]{:S(2)}, u32[]{:S(2)}) %all-to-all-start.2) | async-done | bytes 8224 | tf_op jit(solution)/shard_map/all_to_all | solution.py:389
  101.9 1.0 correct.1
Async XLA Ops:
  0.0 1.0 copy-start
  1.0 9.0 %copy-start.1 = (f32[1,3,16,2048]{3,2,1,0:T(8,128)S(1)}, f32[1,3,16,2048]{3,2,1,0:T(8,128)}, u32[]{:S(2)}) copy-start(f32[1,3,16,2048]{3,2,1,0:T(8,128)} %s_ref.3) | copy-start | bytes 1179652
  1.0 9.0 %copy-start.3 = (f32[256]{0:T(256)S(1)}, f32[256]{0:T(256)}, u32[]{:S(2)}) copy-start(f32[256]{0:T(256)} %param.10) | copy-start | bytes 3076
  1.1 8.9 %collective-permute-start = (f32[4,4,2048]{2,1,0:T(4,128)S(1)}, f32[4,4,2048]{2,1,0:T(4,128)S(1)}, u32[]{:S(2)}, u32[]{:S(2)}) collective-permute-start(f32[4,4,2048]{2,1,0:T(4,128)S(1)} %get-tuple-element.13), channel_id=1, source_target_pairs={{0,1},{1,2},{2,3},{3,4},{4,5},{5,6},{6,7},{7,8},{8,9},{9,10},{10,1... | collective-permute-start | bytes 393224 | tf_op jit(solution)/shard_map/ppermute | solution.py:365
  3.2 6.8 %collective-permute-start.1 = (f32[4,4,2048]{2,1,0:T(4,128)S(1)}, f32[4,4,2048]{2,1,0:T(4,128)S(1)}, u32[]{:S(2)}, u32[]{:S(2)}) collective-permute-start(f32[4,4,2048]{2,1,0:T(4,128)S(1)} %get-tuple-element.14), channel_id=1, source_target_pairs={{1,0},{2,1},{3,2},{4,3},{5,4},{6,5},{7,6},{8,7},{9,8},{10,9},{11,1... | collective-permute-start | bytes 393224 | tf_op jit(solution)/shard_map/ppermute | solution.py:366
  8.2 1.3 %copy-start.2 = (bf16[3,3,256,256]{3,2,1,0:T(8,128)(2,1)S(1)}, bf16[3,3,256,256]{3,2,1,0:T(8,128)(2,1)}, u32[]{:S(2)}) copy-start(bf16[3,3,256,256]{3,2,1,0:T(8,128)(2,1)} %cw_ref.1) | copy-start | bytes 3538948
  14.6 25.8 %all-to-all-start = ((f32[32,8,256]{2,1,0:T(8,128)}), f32[32,8,256]{2,1,0:T(8,128)S(1)}, u32[]{:S(2)}, u32[]{:S(2)}) async-start(f32[32,8,256]{2,1,0:T(8,128)} %get-tuple-element.18), calls=%async_computation | async-start | bytes 524288 | tf_op jit(solution)/shard_map/all_to_all | solution.py:377
  88.6 13.3 %all-to-all-start.2 = ((f32[16,1,128]{2,1,0:T(1,128)}), f32[16,1,128]{2,1,0:T(1,128)S(1)}, u32[]{:S(2)}, u32[]{:S(2)}) async-start(f32[16,1,128]{2,1,0:T(1,128)} %shard_map.64), calls=%async_computation.2 | async-start | bytes 16384 | tf_op jit(solution)/shard_map/all_to_all | solution.py:389

commit v6 on v4

--- a/solution.py
+++ b/solution.py
@@ -175,7 +175,7 @@
             out_ref[n, :, 32 * f:32 * f + 32] = gt[4 * n + f:4 * n + f + 1, :]
         out_ref[n, :, 96:128] = jnp.zeros((1, 32), f32)
 
-SPLITS = (0, 19, 18, 17, 16, 15, 14, 13, 17, 16, 15, 14, 20, 19, 18, 17)
+SPLITS = (0, 18, 17, 16, 15, 14, 13, 12, 18, 17, 16, 15, 20, 19, 18, 17)
 
 def chain(recv, wt, lw, ow, cb, SPLITS=SPLITS, PIECE=384, ROLL=False):
     L = ROWS * W1

time: 102 us -> 102 us (level)
  no operation moved by 1% of the time
where the time goes in v6:
time: 102 us; the launch traced here: 101 us
  blocking collectives  35.2 us (35%)
  Pallas kernels  31 us (30%)
  starting transfers between devices  19.4 us (19%)
  waiting for transfers between devices  12.1 us (12%)
  local copies, waits for them, and re-layouts  2.27 us (2%)
  other arithmetic  1.4 us (1%)
    pallas_call x1, Pallas kernels, chain(): pl.pallas_call(functools.partial(chain_kernel, tuple(SPLITS), PIECE, ROLL...  23.3 us
    all_to_all x1, blocking collectives, shards(): recv = lax.all_to_all(send, 'tm', 0, 0)  22.6 us
    all_to_all x1, starting transfers between devices, shards(): c = lax.all_to_all(c, 'space', 0, 0)  13.7 us
    all_to_all x1, blocking collectives, shards(): g = lax.all_to_all(g, 'tm', 0, 0)  12.5 us
    all_to_all x1, waiting for transfers between devices, shards(): c = lax.all_to_all(c, 'space', 0, 0)  12.1 us
    pallas_call x1, Pallas kernels, shards(): pl.pallas_call(first_kernel, out_shape=[jax.ShapeDtypeStruct(slab.shape,...  4.6 us
    ppermute x1, starting transfers between devices, shards(): lax.ppermute(down, 'space', [((i + 1) % count, i) for i in range(count)])  3.64 us
    unnamed x8, local copies, waits for them, and re-layouts  2.27 us
  transfers between devices with their start and end apart: 3, of which 1 were waited for; matrix products, arithmetic and copies ran while one was open for 1% of the time, Pallas kernels for 0%

profile of v6, /device:TPU:2, one launch (start us, length us, event | category | flops | bytes accessed | tf_op | source)
XLA Modules:
  0.0 101.4 jit_solution(14658346851170225072)
XLA Ops:
  0.0 0.0 copy-start
  0.0 1.0 copy-done
  1.0 0.0 copy-start.1
  1.0 0.0 copy-start.3
  1.0 0.1 edges.1
  1.1 2.1 %collective-permute-start = (f32[4,4,2048]{2,1,0:T(4,128)S(1)}, f32[4,4,2048]{2,1,0:T(4,128)S(1)}, u32[]{:S(2)}, u32[]{:S(2)}) collective-permute-start(f32[4,4,2048]{2,1,0:T(4,128)S(1)} %get-tuple-element.12), channel_id=1, source_target_pairs={{0,1},{1,2},{2,3},{3,4},{4,5},{5,6},{6,7},{7,8},{8,9},{9,10},{10,1... | collective-permute-start | bytes 393224 | tf_op jit(solution)/shard_map/ppermute | solution.py:359
  3.2 3.6 %collective-permute-start.1 = (f32[4,4,2048]{2,1,0:T(4,128)S(1)}, f32[4,4,2048]{2,1,0:T(4,128)S(1)}, u32[]{:S(2)}, u32[]{:S(2)}) collective-permute-start(f32[4,4,2048]{2,1,0:T(4,128)S(1)} %get-tuple-element.13), channel_id=1, source_target_pairs={{1,0},{2,1},{3,2},{4,3},{5,4},{6,5},{7,6},{8,7},{9,8},{10,9},{11,1... | collective-permute-start | bytes 393224 | tf_op jit(solution)/shard_map/ppermute | solution.py:360
  6.8 0.7 convert_element_type.3
  7.5 0.7 pad_maximum_fusion.small_ref
  8.2 0.0 copy-start.2
  8.2 1.3 %copy-done.2 = bf16[3,3,256,256]{3,2,1,0:T(8,128)(2,1)S(1)} copy-done((bf16[3,3,256,256]{3,2,1,0:T(8,128)(2,1)S(1)}, bf16[3,3,256,256]{3,2,1,0:T(8,128)(2,1)}, u32[]{:S(2)}) %copy-start.2) | copy-done | bytes 1179672
  9.5 0.5 tables.1
  10.0 0.0 collective-permute-done.up_ref
  10.0 0.0 collective-permute-done.1.dn_ref
  10.0 0.0 copy-done.1
  10.0 0.0 copy-done.3
  10.0 4.6 %fine_and_guess.1 = (f32[3,16,2048]{2,1,0:T(8,128)S(1)}, f32[32,8,256]{2,1,0:T(8,128)}) custom-call(s32[1]{0:T(128)} %bitcast.1.tm_ref, f32[1,3,16,2048]{3,2,1,0:T(8,128)S(1)} %copy-done.1, f32[4,4,2048]{2,1,0:T(4,128)S(1)} %collective-permute-done.up_ref, f32[4,4,2048]{2,1,0:T(4,128)S(1)} %collective-permute-done.1.dn_ref, ...), custom_call_target="tpu_custom_call" | custom-call | tf_op jit(solution)/shard_map/fine_and_guess/pallas_call | solution.py:364
  14.6 13.7 %all-to-all-start = ((f32[32,8,256]{2,1,0:T(8,128)}), f32[32,8,256]{2,1,0:T(8,128)S(1)}, u32[]{:S(2)}, u32[]{:S(2)}) async-start(f32[32,8,256]{2,1,0:T(8,128)} %get-tuple-element.17), calls=%async_computation | async-start | bytes 524288 | tf_op jit(solution)/shard_map/all_to_all | solution.py:371
  28.3 12.1 %all-to-all-done.b_ref = f32[32,8,256]{2,1,0:T(8,128)S(1)} async-done(((f32[32,8,256]{2,1,0:T(8,128)}), f32[32,8,256]{2,1,0:T(8,128)S(1)}, u32[]{:S(2)}, u32[]{:S(2)}) %all-to-all-start) | async-done | bytes 262176 | tf_op jit(solution)/shard_map/all_to_all | solution.py:371
  40.4 1.6 %windows.1 = f32[16,4,1152]{2,1,0:T(4,128)S(1)} custom-call(s32[1]{0:T(128)} %bitcast.sp_ref, f32[32,8,256]{2,1,0:T(8,128)S(1)} %all-to-all-done.b_ref), custom_call_target="tpu_custom_call" | custom-call | tf_op jit(solution)/shard_map/windows/pallas_call | solution.py:372
  42.0 22.6 %all_to_all.15.r_ref = f32[16,4,1152]{2,1,0:T(4,128)S(1)} all-to-all(f32[16,4,1152]{2,1,0:T(4,128)S(1)} %windows.1), channel_id=1, replica_groups=mesh['tm'=16,'space'=32] {'tm'}, dimensions={0} | all-to-all | bytes 589824 | tf_op jit(solution)/shard_map/all_to_all | solution.py:377
  64.6 23.3 %shard_map.64 = f32[16,1,128]{2,1,0:T(1,128)S(1)} custom-call(f32[16,4,1152]{2,1,0:T(4,128)S(1)} %all_to_all.15.r_ref, bf16[3,768,256]{2,1,0:T(8,128)(2,1)S(1)} %get-tuple-element.14.wt_ref, bf16[256,256]{1,0:T(8,128)(2,1)S(1)} %get-tuple-element.15.lw_ref, bf16[256,128]{1,0:T(8,128)(2,1)S(1)} %get-tuple-element.16.ow_ref, f32[1,256]{1,0:T(1,128)S(1)} %bitcast.6), custom_call_target="tpu_custom_call" | custom-call | tf_op jit(solution)/shard_map/pallas_call | solution.py:183
  87.9 12.5 %all_to_all.16.g_ref = f32[16,1,128]{2,1,0:T(1,128)S(1)} all-to-all(f32[16,1,128]{2,1,0:T(1,128)S(1)} %shard_map.64), channel_id=1, replica_groups=mesh['tm'=16,'space'=32] {'tm'}, dimensions={0} | all-to-all | bytes 16384 | tf_op jit(solution)/shard_map/all_to_all | solution.py:379
  100.5 1.0 correct.1
Async XLA Ops:
  0.0 1.0 copy-start
  1.0 9.0 %copy-start.1 = (f32[1,3,16,2048]{3,2,1,0:T(8,128)S(1)}, f32[1,3,16,2048]{3,2,1,0:T(8,128)}, u32[]{:S(2)}) copy-start(f32[1,3,16,2048]{3,2,1,0:T(8,128)} %s_ref.3) | copy-start | bytes 1179652
  1.0 9.0 %copy-start.3 = (f32[256]{0:T(256)S(1)}, f32[256]{0:T(256)}, u32[]{:S(2)}) copy-start(f32[256]{0:T(256)} %param.10) | copy-start | bytes 3076
  1.1 8.9 %collective-permute-start = (f32[4,4,2048]{2,1,0:T(4,128)S(1)}, f32[4,4,2048]{2,1,0:T(4,128)S(1)}, u32[]{:S(2)}, u32[]{:S(2)}) collective-permute-start(f32[4,4,2048]{2,1,0:T(4,128)S(1)} %get-tuple-element.12), channel_id=1, source_target_pairs={{0,1},{1,2},{2,3},{3,4},{4,5},{5,6},{6,7},{7,8},{8,9},{9,10},{10,1... | collective-permute-start | bytes 393224 | tf_op jit(solution)/shard_map/ppermute | solution.py:359
  3.2 6.8 %collective-permute-start.1 = (f32[4,4,2048]{2,1,0:T(4,128)S(1)}, f32[4,4,2048]{2,1,0:T(4,128)S(1)}, u32[]{:S(2)}, u32[]{:S(2)}) collective-permute-start(f32[4,4,2048]{2,1,0:T(4,128)S(1)} %get-tuple-element.13), channel_id=1, source_target_pairs={{1,0},{2,1},{3,2},{4,3},{5,4},{6,5},{7,6},{8,7},{9,8},{10,9},{11,1... | collective-permute-start | bytes 393224 | tf_op jit(solution)/shard_map/ppermute | solution.py:360
  8.2 1.3 %copy-start.2 = (bf16[3,3,256,256]{3,2,1,0:T(8,128)(2,1)S(1)}, bf16[3,3,256,256]{3,2,1,0:T(8,128)(2,1)}, u32[]{:S(2)}) copy-start(bf16[3,3,256,256]{3,2,1,0:T(8,128)(2,1)} %cw_ref.1) | copy-start | bytes 3538948
  14.6 25.8 %all-to-all-start = ((f32[32,8,256]{2,1,0:T(8,128)}), f32[32,8,256]{2,1,0:T(8,128)S(1)}, u32[]{:S(2)}, u32[]{:S(2)}) async-start(f32[32,8,256]{2,1,0:T(8,128)} %get-tuple-element.17), calls=%async_computation | async-start | bytes 524288 | tf_op jit(solution)/shard_map/all_to_all | solution.py:371
